TPU v7x, 1024 devices: a whole 8x8x8 slice. The times are simulated.
1024 devices in a mesh: tensor: 8 (over y_hi, core), context: 64 (over z, x), dp: 2 (over y_lo).
Axes of the slice: x: 8, y: 8 (y_hi: 4, y_lo: 2; y = y_hi * 2 + y_lo), z: 8, core: 2. Of those that a mesh axis runs over, the one named last changes fastest.
Arguments:
- queries: bfloat16 [2, 8192, 4096], P('dp', 'context', 'tensor'), may hold values from -6 to 6
- key_gates: bfloat16 [2, 8192, 4096], P('dp', 'context', 'tensor'), may hold values from -6 to 6
- values: bfloat16 [2, 8192, 4096], P('dp', 'context', 'tensor'), may hold values from -6 to 6
- out_grad: bfloat16 [2, 8192, 4096], P('dp', 'context', 'tensor'), may hold values from -6 to 6
- featurizer: bfloat16 [3, 3, 4096], P(None, None, 'tensor'), may hold values from -3.5 to 3.5
- long_filter: bfloat16 [8192, 4096], P('context', 'tensor'), may hold values from -2 to 2
Outputs:
- output: bfloat16 [2, 8192, 4096], P('dp', 'context', 'tensor')
- grad_queries: bfloat16 [2, 8192, 4096], P('dp', 'context', 'tensor')
- grad_keys: bfloat16 [2, 8192, 4096], P('dp', 'context', 'tensor')
- grad_values: bfloat16 [2, 8192, 4096], P('dp', 'context', 'tensor')
- grad_long: bfloat16 [8192, 4096], P('context', 'tensor')
All inputs are finite; a program needn't handle non-finite values.
Results may differ from a plain program's by a relative error of at most 0.015.
Values may be sent and summed in bfloat16 or wider, within the bound.
A program may use at most 32 MiB of HBM per device.

v0:
```python
import math

import jax
import jax.numpy as jnp
from jax import lax
from jax.sharding import PartitionSpec as P


def from_behind(block, axis, distance):
    devices = range(lax.axis_size(axis))
    route = [(i - distance, i) for i in devices if i - distance in devices]
    return lax.ppermute(block, axis, route)


def apply_taps(extended, tap_rows, along_axis, length, forward):
    tap_count = tap_rows.shape[0]
    tap_total = None
    for lag in range(tap_count):
        slice_start = tap_count - 1 - lag if forward else lag
        tap_piece = lax.slice_in_dim(extended, slice_start, slice_start + length, axis=along_axis)
        tap_term = tap_rows[lag] * tap_piece
        tap_total = tap_term if tap_total is None else tap_total + tap_term
    return tap_total


def dft_table(length, rows, columns, direction):
    first = jnp.arange(rows, dtype=jnp.int32)
    second = jnp.arange(columns, dtype=jnp.int32)
    product = first[:, None] * second[None, :] % length
    angle = 2.0 * math.pi / length * product.astype(jnp.float32)
    return (jnp.cos(angle), direction * jnp.sin(angle))


def factor_sizes(length):
    chosen = 1
    for option in range(1, math.isqrt(2 * length) + 1):
        if length % option == 0:
            chosen = option
    return (chosen, 2 * length // chosen)


def contract(form, left, right):
    return jnp.einsum(form, left, right, precision=lax.Precision.HIGHEST)


def forward_spectrum(signal):
    rows, length = signal.shape
    inner, outer = factor_sizes(length)
    half = outer // 2
    grid = signal.reshape(rows, half, inner)
    first_cos, first_sin = dft_table(outer, half, outer, -1.0)
    section_real = contract("rqp,qk->rkp", grid, first_cos)
    section_imag = contract("rqp,qk->rkp", grid, first_sin)
    twist_cos, twist_sin = dft_table(2 * length, outer, inner, -1.0)
    turned_real = section_real * twist_cos - section_imag * twist_sin
    turned_imag = section_real * twist_sin + section_imag * twist_cos
    second_cos, second_sin = dft_table(inner, inner, inner, -1.0)
    final_real = contract("rkp,pj->rkj", turned_real, second_cos) - contract(
        "rkp,pj->rkj", turned_imag, second_sin
    )
    final_imag = contract("rkp,pj->rkj", turned_real, second_sin) + contract(
        "rkp,pj->rkj", turned_imag, second_cos
    )
    return (final_real, final_imag)


def inverse_spectrum(spec_real, spec_imag, length):
    rows = spec_real.shape[0]
    inner, outer = factor_sizes(length)
    half = outer // 2
    second_cos, second_sin = dft_table(inner, inner, inner, 1.0)
    section_real = contract("rkj,jp->rkp", spec_real, second_cos) - contract(
        "rkj,jp->rkp", spec_imag, second_sin
    )
    section_imag = contract("rkj,jp->rkp", spec_real, second_sin) + contract(
        "rkj,jp->rkp", spec_imag, second_cos
    )
    twist_cos, twist_sin = dft_table(2 * length, outer, inner, 1.0)
    turned_real = section_real * twist_cos - section_imag * twist_sin
    turned_imag = section_real * twist_sin + section_imag * twist_cos
    first_cos, first_sin = dft_table(outer, outer, half, 1.0)
    final_real = contract("rkp,kq->rqp", turned_real, first_cos) - contract(
        "rkp,kq->rqp", turned_imag, first_sin
    )
    final_imag = contract("rkp,kq->rqp", turned_real, first_sin) + contract(
        "rkp,kq->rqp", turned_imag, first_cos
    )
    return (final_real.reshape(rows, length), final_imag.reshape(rows, length))


def long_terms(signal, filt_rows, signal_grad):
    rows, length = signal.shape
    scale = 1.0 / (2 * length)
    stacked = jnp.concatenate([signal, filt_rows, signal_grad], axis=0).astype(jnp.float32)
    spec_real, spec_imag = forward_spectrum(stacked)
    sig_real, filt_real, grad_real = (
        spec_real[:rows],
        spec_real[rows : 2 * rows],
        spec_real[2 * rows :],
    )
    sig_imag, filt_imag, grad_imag = (
        spec_imag[:rows],
        spec_imag[rows : 2 * rows],
        spec_imag[2 * rows :],
    )
    ahead_real = sig_real * filt_real - sig_imag * filt_imag
    ahead_imag = sig_real * filt_imag + sig_imag * filt_real
    behind_real = grad_real * filt_real + grad_imag * filt_imag
    behind_imag = grad_imag * filt_real - grad_real * filt_imag
    cross_real = grad_real * sig_real + grad_imag * sig_imag
    cross_imag = grad_imag * sig_real - grad_real * sig_imag
    joined_real = jnp.concatenate([ahead_real - behind_imag, cross_real], axis=0)
    joined_imag = jnp.concatenate([ahead_imag + behind_real, cross_imag], axis=0)
    back_real, back_imag = inverse_spectrum(joined_real, joined_imag, length)
    return (back_real[:rows] * scale, back_imag[:rows] * scale, back_real[rows:] * scale)


def on_device(queries, key_gates, values, out_grad, featurizer, long_filter):
    query_rows = queries[0]
    key_rows = key_gates[0]
    value_rows = values[0]
    grad_rows = out_grad[0]
    tap_count = featurizer.shape[1]
    tokens = query_rows.shape[0]
    feat_wide = featurizer.astype(jnp.float32)
    rim_query, rim_key, rim_value = from_behind(
        (
            query_rows[tokens - (tap_count - 1) :],
            key_rows[tokens - (tap_count - 1) :],
            value_rows[tokens - (tap_count - 1) :],
        ),
        "context",
        1,
    )

    def featured(rim_rows, rows, which):
        extended = jnp.concatenate([rim_rows, rows], axis=0).astype(jnp.float32)
        return (
            apply_taps(extended, feat_wide[which], 0, tokens, True)
            .astype(jnp.bfloat16)
            .astype(jnp.float32)
        )

    query_feat = featured(rim_query, query_rows, 0)
    key_feat = featured(rim_key, key_rows, 1)
    value_features = featured(rim_value, value_rows, 2)
    grad_wide = grad_rows.astype(jnp.float32)
    gated = (key_feat * value_features).astype(jnp.bfloat16)
    signal_grad = (grad_wide * query_feat).astype(jnp.bfloat16)
    arrived = (
        lax.all_to_all(gated.T, "context", split_axis=0, concat_axis=1, tiled=True),
        lax.all_to_all(long_filter.T, "context", split_axis=0, concat_axis=1, tiled=True),
        lax.all_to_all(signal_grad.T, "context", split_axis=0, concat_axis=1, tiled=True),
    )
    conv_part, back_part, filter_part = long_terms(arrived[0], arrived[1], arrived[2])
    conv_cols, back_cols = (
        lax.all_to_all(
            conv_part.astype(jnp.bfloat16), "context", split_axis=1, concat_axis=0, tiled=True
        ),
        lax.all_to_all(
            back_part.astype(jnp.bfloat16), "context", split_axis=1, concat_axis=0, tiled=True
        ),
    )
    conv_wide = conv_cols.T.astype(jnp.float32)
    back_wide = back_cols.T.astype(jnp.float32)
    output = (query_feat * conv_wide).astype(jnp.bfloat16)[None]
    query_feat_grad = (grad_wide * conv_wide).astype(jnp.bfloat16)
    key_feat_grad = (back_wide * value_features).astype(jnp.bfloat16)
    value_feat_grad = (back_wide * key_feat).astype(jnp.bfloat16)
    after_query, after_key, after_value = from_behind(
        (
            query_feat_grad[: tap_count - 1],
            key_feat_grad[: tap_count - 1],
            value_feat_grad[: tap_count - 1],
        ),
        "context",
        -1,
    )

    def unfeatured(rows, after_rows, which):
        extended = jnp.concatenate([rows, after_rows], axis=0).astype(jnp.float32)
        return apply_taps(extended, feat_wide[which], 0, tokens, False).astype(jnp.bfloat16)[None]

    grad_queries = unfeatured(query_feat_grad, after_query, 0)
    grad_keys = unfeatured(key_feat_grad, after_key, 1)
    grad_values = unfeatured(value_feat_grad, after_value, 2)
    filter_sum = lax.psum(filter_part, "dp").astype(jnp.bfloat16)
    filter_cols = lax.all_to_all(filter_sum, "context", split_axis=1, concat_axis=0, tiled=True)
    grad_long = filter_cols.T
    return (output, grad_queries, grad_keys, grad_values, grad_long)


def solution(mesh):
    in_specs = (
        P("dp", "context", "tensor"),
        P("dp", "context", "tensor"),
        P("dp", "context", "tensor"),
        P("dp", "context", "tensor"),
        P(None, None, "tensor"),
        P("context", "tensor"),
    )
    out_specs = (
        P("dp", "context", "tensor"),
        P("dp", "context", "tensor"),
        P("dp", "context", "tensor"),
        P("dp", "context", "tensor"),
        P("context", "tensor"),
    )
    return jax.shard_map(
        on_device, mesh=mesh, in_specs=in_specs, out_specs=out_specs, check_vma=False
    )
```

profile of v0, /device:TPU:112, one launch (start us, length us, event | category | flops | bytes accessed | tf_op | source)
XLA Modules:
  0.0 164.7 jit_solution(148673345950852285)
XLA Ops:
  0.7 1.1 copy.32
  1.9 3.4 %collective-permute-start.1 = (bf16[2,512]{0,1:T(8,128)(2,1)S(1)}, bf16[2,512]{0,1:T(8,128)(2,1)S(1)}, u32[]{:S(2)}, u32[]{:S(2)}) collective-permute-start(bf16[2,512]{0,1:T(8,128)(2,1)S(1)} %slice_bitcast_fusion.1), channel_id=1, source_target_pairs={{0,2},{2,4},{4,6},{6,8},{8,10},{10,12},{12,14},{14,16},{16,18},{18... | collective-permute-start | bytes 6152 | tf_op jit(solution)/shard_map/ppermute | solution.py:12
  5.3 1.0 copy.34
  6.4 3.4 %collective-permute-start.2 = (bf16[2,512]{0,1:T(8,128)(2,1)S(1)}, bf16[2,512]{0,1:T(8,128)(2,1)S(1)}, u32[]{:S(2)}, u32[]{:S(2)}) collective-permute-start(bf16[2,512]{0,1:T(8,128)(2,1)S(1)} %slice_bitcast_fusion), channel_id=1, source_target_pairs={{0,2},{2,4},{4,6},{6,8},{8,10},{10,12},{12,14},{14,16},{16,18},{18... | collective-permute-start | bytes 6152 | tf_op jit(solution)/shard_map/ppermute | solution.py:12
  9.8 1.0 copy.30
  11.0 3.4 %collective-permute-start = (bf16[2,512]{0,1:T(8,128)(2,1)S(1)}, bf16[2,512]{0,1:T(8,128)(2,1)S(1)}, u32[]{:S(2)}, u32[]{:S(2)}) collective-permute-start(bf16[2,512]{0,1:T(8,128)(2,1)S(1)} %slice_bitcast_fusion.2), channel_id=1, source_target_pairs={{0,2},{2,4},{4,6},{6,8},{8,10},{10,12},{12,14},{14,16},{16,18},{18... | collective-permute-start | bytes 6152 | tf_op jit(solution)/shard_map/ppermute | solution.py:12
  15.1 19.9 %all-to-all-start.1 = ((bf16[64,8,128]{2,1,0:T(8,128)(2,1)}), bf16[64,8,128]{2,1,0:T(8,128)(2,1)S(1)}, u32[]{:S(2)}, u32[]{:S(2)}) async-start(bf16[64,8,128]{2,1,0:T(8,128)(2,1)} %bitcast.21), calls=%async_computation.1 | async-start | bytes 262144 | tf_op jit(solution)/shard_map/all_to_all | solution.py:152
  35.5 1.4 fusion.53
  36.9 10.8 %all-to-all-done.1 = bf16[64,8,128]{2,1,0:T(8,128)(2,1)S(1)} async-done(((bf16[64,8,128]{2,1,0:T(8,128)(2,1)}), bf16[64,8,128]{2,1,0:T(8,128)(2,1)S(1)}, u32[]{:S(2)}, u32[]{:S(2)}) %all-to-all-start.1) | async-done | bytes 131104 | tf_op jit(solution)/shard_map/all_to_all | solution.py:152
  47.8 4.6 %all-to-all-start = ((bf16[64,8,128]{2,1,0:T(8,128)(2,1)}), bf16[64,8,128]{2,1,0:T(8,128)(2,1)S(1)}, u32[]{:S(2)}, u32[]{:S(2)}) async-start(bf16[64,8,128]{2,1,0:T(8,128)(2,1)} %get-tuple-element.15), calls=%async_computation | async-start | bytes 262144 | tf_op jit(solution)/shard_map/all_to_all | solution.py:151
  52.6 1.1 fusion.52
  53.6 11.5 %all-to-all-done = bf16[64,8,128]{2,1,0:T(8,128)(2,1)S(1)} async-done(((bf16[64,8,128]{2,1,0:T(8,128)(2,1)}), bf16[64,8,128]{2,1,0:T(8,128)(2,1)S(1)}, u32[]{:S(2)}, u32[]{:S(2)}) %all-to-all-start) | async-done | bytes 131104 | tf_op jit(solution)/shard_map/all_to_all | solution.py:151
  65.1 4.8 %all-to-all-start.2 = ((bf16[64,8,128]{2,1,0:T(8,128)(2,1)}), bf16[64,8,128]{2,1,0:T(8,128)(2,1)S(1)}, u32[]{:S(2)}, u32[]{:S(2)}) async-start(bf16[64,8,128]{2,1,0:T(8,128)(2,1)} %get-tuple-element.18), calls=%async_computation.2 | async-start | bytes 262144 | tf_op jit(solution)/shard_map/all_to_all | solution.py:153
  70.5 11.9 %all-to-all-done.2 = bf16[64,8,128]{2,1,0:T(8,128)(2,1)S(1)} async-done(((bf16[64,8,128]{2,1,0:T(8,128)(2,1)}), bf16[64,8,128]{2,1,0:T(8,128)(2,1)S(1)}, u32[]{:S(2)}, u32[]{:S(2)}) %all-to-all-start.2) | async-done | bytes 131104 | tf_op jit(solution)/shard_map/all_to_all | solution.py:153
  84.4 1.7 %fusion.2 = f32[24,128,128]{2,1,0:T(8,128)S(1)} fusion(f32[128,24,128]{2,0,1:T(8,128)S(1)} %fusion.47, f32[128,24,128]{2,0,1:T(8,128)S(1)} %fusion.48, f32[128,128]{1,0:T(8,128)S(1)} %get-tuple-element.38, f32[128,128]{1,0:T(8,128)S(1)} %get-tuple-element.39), kind=kOutput, calls=%fused_computation.2 | convolution fusion | flops 605405184 | bytes 4849664 | tf_op jit(solution)/shard_map/rkp,pj->rkj/dot_general | solution.py:43
  86.1 1.7 %fusion = f32[24,128,128]{2,1,0:T(8,128)S(1)} fusion(f32[128,24,128]{2,0,1:T(8,128)S(1)} %fusion.47, f32[128,24,128]{2,0,1:T(8,128)S(1)} %fusion.48, f32[128,128]{1,0:T(8,128)S(1)} %get-tuple-element.38, f32[128,128]{1,0:T(8,128)S(1)} %get-tuple-element.39), kind=kOutput, calls=%fused_computation | convolution fusion | flops 605388800 | bytes 4849664 | tf_op jit(solution)/shard_map/rkp,pj->rkj/dot_general | solution.py:43
  87.8 1.8 %fusion.8 = f32[24,128,128]{2,1,0:T(8,128)S(1)} fusion(f32[24,128,128]{2,1,0:T(8,128)S(1)} %fusion.2, f32[128,24,128]{2,0,1:T(8,128)S(1)} %fusion.47, f32[128,24,128]{2,0,1:T(8,128)S(1)} %fusion.48, f32[128,128]{1,0:T(8,128)S(1)} %get-tuple-element.38, f32[128,128]{1,0:T(8,128)S(1)} %get-tuple-element.39), kind=kOutput, calls=%fused_computation.10 | convolution fusion | flops 605782016 | bytes 6422528 | tf_op jit(solution)/shard_map/rkp,pj->rkj/dot_general | solution.py:43
  89.6 1.8 %fusion.11 = f32[24,128,128]{2,1,0:T(8,128)S(1)} fusion(f32[24,128,128]{2,1,0:T(8,128)S(1)} %fusion, f32[128,24,128]{2,0,1:T(8,128)S(1)} %fusion.47, f32[128,24,128]{2,0,1:T(8,128)S(1)} %fusion.48, f32[128,128]{1,0:T(8,128)S(1)} %get-tuple-element.38, f32[128,128]{1,0:T(8,128)S(1)} %get-tuple-element.39), kind=kOutput, calls=%fused_computation.11 | convolution fusion | flops 605798400 | bytes 6422528 | tf_op jit(solution)/shard_map/rkp,pj->rkj/dot_general | solution.py:43
  91.9 1.2 fusion.17
  93.1 1.4 fusion.16
  94.5 1.2 convolution_subtract_fusion
  95.8 1.2 convolution_add_fusion
  100.6 4.6 %all-to-all-start.4 = ((bf16[8,64,128]{2,0,1:T(8,128)(2,1)}), bf16[8,64,128]{2,0,1:T(8,128)(2,1)S(1)}, u32[]{:S(2)}, u32[]{:S(2)}) async-start(bf16[8,64,128]{2,0,1:T(8,128)(2,1)} %copy.42), calls=%async_computation.4 | async-start | bytes 262144 | tf_op jit(solution)/shard_map/all_to_all | solution.py:160
  107.1 10.8 %all-to-all-done.4 = bf16[8,64,128]{2,0,1:T(8,128)(2,1)S(1)} async-done(((bf16[8,64,128]{2,0,1:T(8,128)(2,1)}), bf16[8,64,128]{2,0,1:T(8,128)(2,1)S(1)}, u32[]{:S(2)}, u32[]{:S(2)}) %all-to-all-start.4) | async-done | bytes 131104 | tf_op jit(solution)/shard_map/all_to_all | solution.py:160
  117.9 4.6 %all-to-all-start.3 = ((bf16[8,64,128]{2,0,1:T(8,128)(2,1)}), bf16[8,64,128]{2,0,1:T(8,128)(2,1)S(1)}, u32[]{:S(2)}, u32[]{:S(2)}) async-start(bf16[8,64,128]{2,0,1:T(8,128)(2,1)} %copy.41), calls=%async_computation.3 | async-start | bytes 262144 | tf_op jit(solution)/shard_map/all_to_all | solution.py:157
  122.5 11.5 %all-reduce.1 = bf16[8,8192]{1,0:T(8,128)(2,1)} all-reduce(f32[8,8192]{1,0:T(8,128)S(1)} %bitcast.144), channel_id=1, replica_groups=mesh['tensor'=8,'context'=64,'dp'=2] {'dp'}, use_global_device_ids=true, to_apply=%region_0.1 | all-reduce | flops 65536 | bytes 393216 | tf_op jit(solution)/shard_map/psum | solution.py:187
  134.1 1.2 all-to-all-done.3
  135.2 11.5 %all-to-all-start.5 = ((bf16[8,64,128]{2,0,1:T(8,128)(2,1)}), bf16[8,64,128]{2,0,1:T(8,128)(2,1)S(1)}, u32[]{:S(2)}, u32[]{:S(2)}) async-start(bf16[8,64,128]{2,0,1:T(8,128)(2,1)} %bitcast.127), calls=%async_computation.5 | async-start | bytes 262144 | tf_op jit(solution)/shard_map/all_to_all | solution.py:188
  146.8 1.3 collective-permute-start.5
  148.1 1.3 collective-permute-start.4
  149.5 1.3 collective-permute-start.3
  150.8 8.6 %all-to-all-done.5 = bf16[8,64,128]{2,0,1:T(8,128)(2,1)S(1)} async-done(((bf16[8,64,128]{2,0,1:T(8,128)(2,1)}), bf16[8,64,128]{2,0,1:T(8,128)(2,1)S(1)}, u32[]{:S(2)}, u32[]{:S(2)}) %all-to-all-start.5) | async-done | bytes 131104 | tf_op jit(solution)/shard_map/all_to_all | solution.py:188
  (52 shorter events, 15.4 us)
Async XLA Ops:
  0.6 13.7 %copy-start = (bf16[128,512]{1,0:T(8,128)(2,1)S(1)}, bf16[128,512]{1,0:T(8,128)(2,1)}, u32[]{:S(2)}) copy-start(bf16[128,512]{1,0:T(8,128)(2,1)} %param.11) | copy-start | bytes 393220
  0.6 34.4 %copy-start.2 = (bf16[3,3,512]{2,1,0:T(4,128)(2,1)S(1)}, bf16[3,3,512]{2,1,0:T(4,128)(2,1)}, u32[]{:S(2)}) copy-start(bf16[3,3,512]{2,1,0:T(4,128)(2,1)} %param.10) | copy-start | bytes 27652
  0.7 34.4 %copy-start.1 = (bf16[1,128,512]{2,1,0:T(8,128)(2,1)S(1)}, bf16[1,128,512]{2,1,0:T(8,128)(2,1)}, u32[]{:S(2)}) copy-start(bf16[1,128,512]{2,1,0:T(8,128)(2,1)} %param.9) | copy-start | bytes 393220
  1.9 33.4 %collective-permute-start.1 = (bf16[2,512]{0,1:T(8,128)(2,1)S(1)}, bf16[2,512]{0,1:T(8,128)(2,1)S(1)}, u32[]{:S(2)}, u32[]{:S(2)}) collective-permute-start(bf16[2,512]{0,1:T(8,128)(2,1)S(1)} %slice_bitcast_fusion.1), channel_id=1, source_target_pairs={{0,2},{2,4},{4,6},{6,8},{8,10},{10,12},{12,14},{14,16},{16,18},{18... | collective-permute-start | bytes 6152 | tf_op jit(solution)/shard_map/ppermute | solution.py:12
  6.4 29.0 %collective-permute-start.2 = (bf16[2,512]{0,1:T(8,128)(2,1)S(1)}, bf16[2,512]{0,1:T(8,128)(2,1)S(1)}, u32[]{:S(2)}, u32[]{:S(2)}) collective-permute-start(bf16[2,512]{0,1:T(8,128)(2,1)S(1)} %slice_bitcast_fusion), channel_id=1, source_target_pairs={{0,2},{2,4},{4,6},{6,8},{8,10},{10,12},{12,14},{14,16},{16,18},{18... | collective-permute-start | bytes 6152 | tf_op jit(solution)/shard_map/ppermute | solution.py:12
  11.0 41.5 %collective-permute-start = (bf16[2,512]{0,1:T(8,128)(2,1)S(1)}, bf16[2,512]{0,1:T(8,128)(2,1)S(1)}, u32[]{:S(2)}, u32[]{:S(2)}) collective-permute-start(bf16[2,512]{0,1:T(8,128)(2,1)S(1)} %slice_bitcast_fusion.2), channel_id=1, source_target_pairs={{0,2},{2,4},{4,6},{6,8},{8,10},{10,12},{12,14},{14,16},{16,18},{18... | collective-permute-start | bytes 6152 | tf_op jit(solution)/shard_map/ppermute | solution.py:12
  15.1 32.7 %all-to-all-start.1 = ((bf16[64,8,128]{2,1,0:T(8,128)(2,1)}), bf16[64,8,128]{2,1,0:T(8,128)(2,1)S(1)}, u32[]{:S(2)}, u32[]{:S(2)}) async-start(bf16[64,8,128]{2,1,0:T(8,128)(2,1)} %bitcast.21), calls=%async_computation.1 | async-start | bytes 262144 | tf_op jit(solution)/shard_map/all_to_all | solution.py:152
  47.8 17.3 %all-to-all-start = ((bf16[64,8,128]{2,1,0:T(8,128)(2,1)}), bf16[64,8,128]{2,1,0:T(8,128)(2,1)S(1)}, u32[]{:S(2)}, u32[]{:S(2)}) async-start(bf16[64,8,128]{2,1,0:T(8,128)(2,1)} %get-tuple-element.15), calls=%async_computation | async-start | bytes 262144 | tf_op jit(solution)/shard_map/all_to_all | solution.py:151
  65.1 17.3 %all-to-all-start.2 = ((bf16[64,8,128]{2,1,0:T(8,128)(2,1)}), bf16[64,8,128]{2,1,0:T(8,128)(2,1)S(1)}, u32[]{:S(2)}, u32[]{:S(2)}) async-start(bf16[64,8,128]{2,1,0:T(8,128)(2,1)} %get-tuple-element.18), calls=%async_computation.2 | async-start | bytes 262144 | tf_op jit(solution)/shard_map/all_to_all | solution.py:153
  100.6 17.3 %all-to-all-start.4 = ((bf16[8,64,128]{2,0,1:T(8,128)(2,1)}), bf16[8,64,128]{2,0,1:T(8,128)(2,1)S(1)}, u32[]{:S(2)}, u32[]{:S(2)}) async-start(bf16[8,64,128]{2,0,1:T(8,128)(2,1)} %copy.42), calls=%async_computation.4 | async-start | bytes 262144 | tf_op jit(solution)/shard_map/all_to_all | solution.py:160
  117.9 17.3 %all-to-all-start.3 = ((bf16[8,64,128]{2,0,1:T(8,128)(2,1)}), bf16[8,64,128]{2,0,1:T(8,128)(2,1)S(1)}, u32[]{:S(2)}, u32[]{:S(2)}) async-start(bf16[8,64,128]{2,0,1:T(8,128)(2,1)} %copy.41), calls=%async_computation.3 | async-start | bytes 262144 | tf_op jit(solution)/shard_map/all_to_all | solution.py:157
  135.2 24.2 %all-to-all-start.5 = ((bf16[8,64,128]{2,0,1:T(8,128)(2,1)}), bf16[8,64,128]{2,0,1:T(8,128)(2,1)S(1)}, u32[]{:S(2)}, u32[]{:S(2)}) async-start(bf16[8,64,128]{2,0,1:T(8,128)(2,1)} %bitcast.127), calls=%async_computation.5 | async-start | bytes 262144 | tf_op jit(solution)/shard_map/all_to_all | solution.py:188
  146.8 14.2 %collective-permute-start.5 = (bf16[2,512]{0,1:T(8,128)(2,1)S(1)}, bf16[2,512]{0,1:T(8,128)(2,1)S(1)}, u32[]{:S(2)}, u32[]{:S(2)}) collective-permute-start(bf16[2,512]{0,1:T(8,128)(2,1)S(1)} %bitcast.147), channel_id=1, source_target_pairs={{2,0},{4,2},{6,4},{8,6},{10,8},{12,10},{14,12},{16,14},{18,16},{20... | collective-permute-start | bytes 6152 | tf_op jit(solution)/shard_map/ppermute | solution.py:12
  148.1 13.3 %collective-permute-start.4 = (bf16[2,512]{0,1:T(8,128)(2,1)S(1)}, bf16[2,512]{0,1:T(8,128)(2,1)S(1)}, u32[]{:S(2)}, u32[]{:S(2)}) collective-permute-start(bf16[2,512]{0,1:T(8,128)(2,1)S(1)} %bitcast.145), channel_id=1, source_target_pairs={{2,0},{4,2},{6,4},{8,6},{10,8},{12,10},{14,12},{16,14},{18,16},{20... | collective-permute-start | bytes 6152 | tf_op jit(solution)/shard_map/ppermute | solution.py:12
  149.5 13.9 %collective-permute-start.3 = (bf16[2,512]{0,1:T(8,128)(2,1)S(1)}, bf16[2,512]{0,1:T(8,128)(2,1)S(1)}, u32[]{:S(2)}, u32[]{:S(2)}) collective-permute-start(bf16[2,512]{0,1:T(8,128)(2,1)S(1)} %bitcast.146), channel_id=1, source_target_pairs={{2,0},{4,2},{6,4},{8,6},{10,8},{12,10},{14,12},{16,14},{18,16},{20... | collective-permute-start | bytes 6152 | tf_op jit(solution)/shard_map/ppermute | solution.py:12
where the time goes:
time: 166 us; the launch traced here: 165 us
  starting transfers between devices  64.2 us (39%)
  waiting for transfers between devices  54.8 us (33%)
  matrix products  17.7 us (11%)
  blocking collectives  11.5 us (7%)
  local copies, waits for them, and re-layouts  9.89 us (6%)
  other arithmetic  5.45 us (3%)
    all_to_all x1, starting transfers between devices, on_device(): lax.all_to_all(long_filter.T, 'context', split_axis=0, concat_axis=1, til...  19.9 us
    dot_general x14, matrix products, contract(): return jnp.einsum(form, left, right, precision=lax.Precision.HIGHEST)  17.7 us
    ppermute x6, starting transfers between devices, from_behind(): return lax.ppermute(block, axis, route)  14.1 us
    all_to_all x1, waiting for transfers between devices, on_device(): lax.all_to_all(signal_grad.T, 'context', split_axis=0, concat_axis=1, til...  11.9 us
    all_to_all x1, starting transfers between devices, on_device(): lax.all_to_all(filter_sum, 'context', split_axis=1, concat_axis=0, tiled=...  11.5 us
    psum x1, blocking collectives, on_device(): filter_sum = lax.psum(filter_part, 'dp').astype(jnp.bfloat16)  11.5 us
    all_to_all x1, waiting for transfers between devices, on_device(): lax.all_to_all(gated.T, 'context', split_axis=0, concat_axis=1, tiled=True)  11.5 us
    all_to_all x1, waiting for transfers between devices, on_device(): lax.all_to_all(long_filter.T, 'context', split_axis=0, concat_axis=1, til...  10.8 us
  transfers between devices with their start and end apart: 12, of which 6 were waited for; matrix products, arithmetic and copies ran while one was open for 8% of the time, Pallas kernels for 0%

commit v1 on v0

v1 whole, which is shorter than its diff:
```python
import functools
import math

import ml_dtypes
import numpy as np

import jax
import jax.numpy as jnp
from jax import lax
from jax.experimental import pallas as pl
from jax.experimental.pallas import tpu as pltpu
from jax.sharding import PartitionSpec as P

MESH = pl.DeviceIdType.MESH
F32 = jnp.float32
BF16 = jnp.bfloat16


def tables(blocks, width):
    full = 2 * blocks * width
    a = np.arange(blocks) + 0.5
    q = np.arange(blocks)
    p = np.arange(width)
    angle_qa = 2.0 * math.pi * np.outer(a, q) / (2 * blocks)
    first = np.concatenate([np.cos(angle_qa), -np.sin(angle_qa)], axis=0)
    last = np.concatenate([np.cos(angle_qa.T), -np.sin(angle_qa.T)], axis=1) * (2.0 / full)
    angle_ap = 2.0 * math.pi * np.outer(a, p) / full
    twist = np.stack([np.cos(angle_ap), np.sin(angle_ap)])
    angle_pb = 2.0 * math.pi * (np.outer(p, p) % width) / width
    cos, sin = np.cos(angle_pb), np.sin(angle_pb)
    middle = np.block([[cos, -sin], [sin, cos]])
    half = lambda x: jnp.asarray(x.astype(np.float32).astype(ml_dtypes.bfloat16))
    return (
        half(first),
        half(middle),
        half(middle.T),
        half(last),
        jnp.asarray(twist.astype(np.float32)),
    )


def far_first(step, count):
    up = (step + 1) // 2
    return lax.rem(count // 2 + jnp.where(lax.rem(step, 2) == 1, up, count - step // 2), count)


def main_kernel(
    sizes,
    query_ref,
    key_ref,
    value_ref,
    grad_ref,
    feat_ref,
    filt_ref,
    first_ref,
    middle_ref,
    back_middle_ref,
    last_ref,
    twist_ref,
    conv_out,
    back_out,
    lag_out,
    qf_out,
    kf_out,
    vf_out,
    after_out,
    ext,
    rim_send,
    rim_recv,
    after_send,
    after_recv,
    filt_send,
    filt_recv,
    pair_send,
    pair_recv,
    part_send,
    part_recv,
    conv_send,
    conv_recv,
    lag_send,
    lag_recv,
    wide,
    wide_filt,
    turned,
    filt_spec,
    gate_spec,
    grad_spec,
    product,
    send_sems,
    recv_sems,
):
    ctx, chans, fast = sizes
    tokens, width = query_ref.shape
    me = lax.axis_index("context")
    dp = lax.axis_index("dp")
    slow = ctx // fast
    my_slow, my_fast = me // fast, lax.rem(me, fast)
    following, previous = lax.rem(me + 1, ctx), lax.rem(me + ctx - 1, ctx)
    partner = 1 - dp

    barrier = pltpu.get_barrier_semaphore()

    def peer_of(step):
        s, f = far_first(step // fast, slow), far_first(lax.rem(step, fast), fast)
        return lax.rem(my_slow + s, slow) * fast + lax.rem(my_fast + f, fast)

    @pl.loop(0, ctx - 1)
    def _(step):
        pl.semaphore_signal(
            barrier, inc=1, device_id={"context": peer_of(step)}, device_id_type=MESH
        )

    pl.semaphore_signal(barrier, inc=1, device_id={"dp": partner}, device_id_type=MESH)

    def remote(src, dst, which, device):
        return pltpu.make_async_remote_copy(
            src_ref=src,
            dst_ref=dst,
            send_sem=send_sems.at[which],
            recv_sem=recv_sems.at[which],
            device_id=device,
            device_id_type=MESH,
        )

    def scatter(src, dst, which):
        @pl.loop(0, ctx - 1)
        def _(step):
            peer = peer_of(step)
            remote(src.at[peer], dst.at[me], which, {"context": peer}).start()

        dst[me] = src[me]

    def wait_scatter(ref, sems, which):
        rows = ref.at[pl.ds(0, ctx - 1)]
        pltpu.make_async_copy(rows, rows, sems.at[which]).wait()

    filt_send[...] = filt_ref[...].astype(F32).T.reshape(ctx, chans, tokens).astype(BF16)
    tail = pl.ds(tokens - 8, 8)
    rim_send[0, 0:2] = query_ref[tokens - 16 :].astype(F32)[14:]
    rim_send[0, 2:4] = key_ref[tokens - 16 :].astype(F32)[14:]
    rim_send[0, 4:6] = value_ref[tokens - 16 :].astype(F32)[14:]
    rim_send[0, 6:8] = jnp.zeros((2, width), F32)

    pl.semaphore_wait(barrier, ctx)

    rim_copy = remote(rim_send, rim_recv, 0, {"context": following})
    rim_copy.start()
    scatter(filt_send, filt_recv, 1)
    rim_copy.wait()

    keep = jnp.where(me == 0, 0.0, 1.0).astype(F32)

    def featured(rows_ref, which):
        ext[8 : 8 + tokens] = rows_ref[...].astype(F32)
        ext[6:8] = rim_recv[0, 2 * which : 2 * which + 2] * keep
        total = None
        for lag in range(3):
            tap = feat_ref[which, lag : lag + 1, :]
            term = tap * ext[8 - lag : 8 - lag + tokens]
            total = term if total is None else total + term
        return total.astype(BF16)

    query_feat = featured(query_ref, 0)
    qf_out[...] = query_feat
    key_feat = featured(key_ref, 1)
    kf_out[...] = key_feat
    value_feat = featured(value_ref, 2)
    vf_out[...] = value_feat
    gated = (key_feat.astype(F32) * value_feat.astype(F32)).T.reshape(ctx, chans, tokens)
    signal = (grad_ref[...].astype(F32) * query_feat.astype(F32)).T.reshape(ctx, chans, tokens)
    pair_send[...] = jnp.concatenate([gated, signal], axis=1).astype(BF16)
    scatter(pair_send, pair_recv, 2)

    def spectra(wide_ref, rows, start, dest):
        for channel in range(chans):
            grid = wide_ref[pl.ds(start + channel, ctx, stride=rows), :].astype(BF16)
            section = jnp.dot(first_ref[...], grid, preferred_element_type=F32)
            real, imag = section[:ctx], section[ctx:]
            cos, sin = twist_ref[0], twist_ref[1]
            here = pl.ds(channel * ctx, ctx)
            turned[here, 0:tokens] = (real * cos + imag * sin).astype(BF16)
            turned[here, tokens : 2 * tokens] = (imag * cos - real * sin).astype(BF16)
        dest[...] = jnp.dot(turned[...], middle_ref[...], preferred_element_type=F32)

    wait_scatter(filt_recv, recv_sems, 1)
    wide_filt[...] = filt_recv[...].astype(F32).reshape(ctx * chans, tokens)
    spectra(wide_filt, chans, 0, filt_spec)
    wait_scatter(pair_recv, recv_sems, 2)
    wide[...] = pair_recv[...].astype(F32).reshape(ctx * 2 * chans, tokens)
    spectra(wide, 2 * chans, 0, gate_spec)
    spectra(wide, 2 * chans, chans, grad_spec)

    def parts(ref):
        return ref[:, 0:tokens], ref[:, tokens : 2 * tokens]

    def inverse(real, imag, wide_ref, rows, start):
        product[:, 0:tokens] = real.astype(BF16)
        product[:, tokens : 2 * tokens] = imag.astype(BF16)
        gate = jnp.dot(product[...], back_middle_ref[...], preferred_element_type=F32)
        cos, sin = twist_ref[0], twist_ref[1]
        for channel in range(chans):
            piece = gate[channel * ctx : (channel + 1) * ctx]
            real, imag = piece[:, :tokens], piece[:, tokens:]
            stacked = jnp.concatenate([real * cos - imag * sin, imag * cos + real * sin], axis=0)
            wide_ref[pl.ds(start + channel, ctx, stride=rows), :] = jnp.dot(
                last_ref[...], stacked.astype(BF16), preferred_element_type=F32
            )

    gate_real, gate_imag = parts(gate_spec)
    grad_real, grad_imag = parts(grad_spec)
    inverse(
        grad_real * gate_real + grad_imag * gate_imag,
        grad_imag * gate_real - grad_real * gate_imag,
        wide_filt,
        chans,
        0,
    )
    part_send[...] = wide_filt[...].reshape(ctx, chans, tokens).astype(BF16)
    part_copy = remote(part_send, part_recv, 3, {"dp": partner})
    part_copy.start()
    filt_real, filt_imag = parts(filt_spec)
    gate_real, gate_imag = parts(gate_spec)
    inverse(
        gate_real * filt_real - gate_imag * filt_imag,
        gate_real * filt_imag + gate_imag * filt_real,
        wide,
        2 * chans,
        0,
    )
    filt_real, filt_imag = parts(filt_spec)
    grad_real, grad_imag = parts(grad_spec)
    inverse(
        grad_real * filt_real + grad_imag * filt_imag,
        grad_imag * filt_real - grad_real * filt_imag,
        wide,
        2 * chans,
        chans,
    )
    conv_send[...] = wide[...].reshape(ctx, 2 * chans, tokens).astype(BF16)
    scatter(conv_send, conv_recv, 4)
    part_copy.wait()
    lag_send[...] = (part_send[...].astype(F32) + part_recv[...].astype(F32)).astype(BF16)
    scatter(lag_send, lag_recv, 5)

    wait_scatter(conv_recv, recv_sems, 4)
    both = conv_recv[...].astype(F32)
    conv = both[:, :chans].reshape(width, tokens).T
    back = both[:, chans:].reshape(width, tokens).T
    conv_out[...] = conv.astype(BF16)
    back_out[...] = back.astype(BF16)

    def rounded(x):
        return x.astype(BF16).astype(F32)

    head = 16
    after_send[0, 0:2] = rounded(grad_ref[:head].astype(F32) * conv[:head])[:2]
    after_send[0, 2:4] = rounded(vf_out[:head].astype(F32) * back[:head])[:2]
    after_send[0, 4:6] = rounded(kf_out[:head].astype(F32) * back[:head])[:2]
    after_send[0, 6:8] = jnp.zeros((2, width), F32)
    after_copy = remote(after_send, after_recv, 6, {"context": previous})
    after_copy.start()
    wait_scatter(lag_recv, recv_sems, 5)
    lag_out[...] = lag_recv[...].astype(F32).reshape(width, tokens).T.astype(BF16)
    after_copy.wait()
    after_out[...] = after_recv[0] * jnp.where(me == ctx - 1, 0.0, 1.0).astype(F32)
    wait_scatter(filt_send, send_sems, 1)
    wait_scatter(pair_send, send_sems, 2)
    wait_scatter(conv_send, send_sems, 4)
    wait_scatter(lag_send, send_sems, 5)


def final_kernel(
    conv_ref,
    back_ref,
    lag_ref,
    grad_ref,
    qf_ref,
    kf_ref,
    vf_ref,
    after_ref,
    feat_ref,
    out_ref,
    gq_ref,
    gk_ref,
    gv_ref,
    lag_out,
    ext,
):
    tokens = conv_ref.shape[0]
    conv = conv_ref[...].astype(F32)
    back = back_ref[...].astype(F32)
    out_ref[0] = (qf_ref[...].astype(F32) * conv).astype(BF16)

    def unfeatured(rows, which, dest):
        ext[0:tokens] = rows.astype(BF16).astype(F32)
        ext[tokens : tokens + 2] = after_ref[2 * which : 2 * which + 2]
        total = None
        for lag in range(3):
            term = feat_ref[which, lag : lag + 1, :] * ext[lag : lag + tokens]
            total = term if total is None else total + term
        dest[0] = total.astype(BF16)

    unfeatured(grad_ref[...].astype(F32) * conv, 0, gq_ref)
    unfeatured(back * vf_ref[...].astype(F32), 1, gk_ref)
    unfeatured(back * kf_ref[...].astype(F32), 2, gv_ref)
    lag_out[...] = lag_ref[...]


def on_device(ctx, queries, key_gates, values, out_grad, featurizer, long_filter):
    tokens, width = long_filter.shape
    chans = width // ctx
    fast = 8
    consts = tables(ctx, tokens)
    taps = featurizer.astype(F32)
    vmem = pl.BlockSpec(memory_space=pltpu.VMEM)
    like = lambda *shape, dtype=BF16: jax.ShapeDtypeStruct(shape, dtype)
    buf = lambda *shape, dtype=BF16: pltpu.VMEM(shape, dtype)
    results = pl.pallas_call(
        functools.partial(main_kernel, (ctx, chans, fast)),
        out_shape=(
            like(tokens, width),
            like(tokens, width),
            like(tokens, width),
            like(tokens, width),
            like(tokens, width),
            like(tokens, width),
            like(8, width, dtype=F32),
        ),
        in_specs=[vmem] * 11,
        out_specs=(vmem,) * 7,
        scratch_shapes=[
            buf(tokens + 16, width, dtype=F32),
            buf(1, 8, width, dtype=F32),
            buf(1, 8, width, dtype=F32),
            buf(1, 8, width, dtype=F32),
            buf(1, 8, width, dtype=F32),
            buf(ctx, chans, tokens),
            buf(ctx, chans, tokens),
            buf(ctx, 2 * chans, tokens),
            buf(ctx, 2 * chans, tokens),
            buf(ctx, chans, tokens),
            buf(ctx, chans, tokens),
            buf(ctx, 2 * chans, tokens),
            buf(ctx, 2 * chans, tokens),
            buf(ctx, chans, tokens),
            buf(ctx, chans, tokens),
            buf(ctx * 2 * chans, tokens, dtype=F32),
            buf(ctx * chans, tokens, dtype=F32),
            buf(ctx * chans, 2 * tokens),
            buf(ctx * chans, 2 * tokens, dtype=F32),
            buf(ctx * chans, 2 * tokens, dtype=F32),
            buf(ctx * chans, 2 * tokens, dtype=F32),
            buf(ctx * chans, 2 * tokens),
            pltpu.SemaphoreType.DMA((7,)),
            pltpu.SemaphoreType.DMA((7,)),
        ],
        compiler_params=pltpu.CompilerParams(
            collective_id=0, has_side_effects=True, vmem_limit_bytes=48 * 1024 * 1024
        ),
        name="exchange",
    )(queries[0], key_gates[0], values[0], out_grad[0], taps, long_filter, *consts)
    conv, back, lag, qf, kf, vf, after = results
    return pl.pallas_call(
        final_kernel,
        out_shape=(like(1, tokens, width),) * 4 + (like(tokens, width),),
        in_specs=[vmem] * 9,
        out_specs=(vmem,) * 5,
        scratch_shapes=[buf(tokens + 16, width, dtype=F32)],
        compiler_params=pltpu.CompilerParams(vmem_limit_bytes=32 * 1024 * 1024),
        name="finish",
    )(conv, back, lag, out_grad[0], qf, kf, vf, after, taps)


def solution(mesh):
    in_specs = (
        P("dp", "context", "tensor"),
        P("dp", "context", "tensor"),
        P("dp", "context", "tensor"),
        P("dp", "context", "tensor"),
        P(None, None, "tensor"),
        P("context", "tensor"),
    )
    out_specs = (
        P("dp", "context", "tensor"),
        P("dp", "context", "tensor"),
        P("dp", "context", "tensor"),
        P("dp", "context", "tensor"),
        P("context", "tensor"),
    )
    return jax.shard_map(
        functools.partial(on_device, mesh.shape["context"]),
        mesh=mesh,
        in_specs=in_specs,
        out_specs=out_specs,
        check_vma=False,
    )
```

time: 166 us -> 59.7 us (0.36)
  starting transfers between devices: 64.2 us -> 0 us
  waiting for transfers between devices: 54.8 us -> 0 us
  Pallas kernels: 0 us -> 50.7 us
  matrix products: 17.7 us -> 0 us
  blocking collectives: 11.5 us -> 0 us
  other arithmetic: 5.45 us -> 0.72 us
  local copies, waits for them, and re-layouts: 9.89 us -> 7.21 us
    all_to_all x6 -> x0, waiting for transfers between devices: 54.8 us -> none  [the longest x1 11.9 us: on_device(): lax.all_to_all(signal_grad.T, 'context', split_axis=0, concat_axis=1, til...]
    pallas_call x0 -> x2, Pallas kernels: none -> 50.7 us  [the longest x1 49.5 us: on_device(): pl.pallas_call(functools.partial(main_kernel, (ctx, chans, fast)), out_sh...]
    all_to_all x6 -> x0, starting transfers between devices: 50.1 us -> none  [the longest x1 19.9 us: on_device(): lax.all_to_all(long_filter.T, 'context', split_axis=0, concat_axis=1, til...]
    dot_general x14 -> x0, matrix products: 17.7 us -> none  [contract(): return jnp.einsum(form, left, right, precision=lax.Precision.HIGHEST)]
    ppermute x6 -> x0, starting transfers between devices: 14.1 us -> none  [from_behind(): return lax.ppermute(block, axis, route)]
    psum x1 -> x0, blocking collectives: 11.5 us -> none  [on_device(): filter_sum = lax.psum(filter_part, 'dp').astype(jnp.bfloat16)]
    all_to_all x2 -> x0, other arithmetic: 2.47 us -> none  [the longest x1 1.4 us: on_device(): lax.all_to_all(gated.T, 'context', split_axis=0, concat_axis=1, tiled=True)]
    unnamed x17 -> x20, local copies, waits for them, and re-layouts: 8.01 us -> 7.21 us
  transfers between devices with their start and end apart: 12 -> 0, of which waited for: 6 -> 0; matrix products, arithmetic and copies ran while one was open for 8% -> 0% of each run, Pallas kernels for 0% -> 0%
where the time goes in v1:
time: 59.7 us; the launch traced here: 59.3 us
  Pallas kernels  50.7 us (85%)
  local copies, waits for them, and re-layouts  7.21 us (12%)
  other arithmetic  0.72 us (1%)
  between operations  0.66 us (1%)
    pallas_call x1, Pallas kernels, on_device(): pl.pallas_call(functools.partial(main_kernel, (ctx, chans, fast)), out_sh...  49.5 us
    unnamed x20, local copies, waits for them, and re-layouts  7.21 us
    pallas_call x1, Pallas kernels, on_device(): pl.pallas_call(final_kernel, out_shape=(like(1, tokens, width),) * 4 + (l...  1.23 us

profile of v1, /device:TPU:112, one launch (start us, length us, event | category | flops | bytes accessed | tf_op | source)
XLA Modules:
  0.0 59.3 jit_solution(2863346996874757446)
XLA Ops:
  0.6 0.0 copy-start.9
  0.6 0.0 copy-start.8
  0.7 0.7 %convert_element_type.3.feat_ref = f32[3,3,512]{2,1,0:T(4,128)S(1)} convert(bf16[3,3,512]{2,1,0:T(4,128)(2,1)} %param.15) | non-fusion elementwise | flops 4608 | bytes 27648 | tf_op jit(solution)/shard_map/convert_element_type | solution.py:314
  1.4 0.0 copy-done.9
  1.4 0.0 copy-done.8
  1.4 0.0 copy-start
  1.4 0.9 %copy-done = bf16[1,128,512]{2,1,0:T(8,128)(2,1)S(1)} copy-done((bf16[1,128,512]{2,1,0:T(8,128)(2,1)S(1)}, bf16[1,128,512]{2,1,0:T(8,128)(2,1)}, u32[]{:S(2)}) %copy-start) | copy-done | bytes 131096
  2.3 0.0 copy-start.1
  2.3 0.9 %copy-done.1 = bf16[1,128,512]{2,1,0:T(8,128)(2,1)S(1)} copy-done((bf16[1,128,512]{2,1,0:T(8,128)(2,1)S(1)}, bf16[1,128,512]{2,1,0:T(8,128)(2,1)}, u32[]{:S(2)}) %copy-start.1) | copy-done | bytes 131096
  3.2 0.0 copy-start.2
  3.2 0.9 %copy-done.2 = bf16[1,128,512]{2,1,0:T(8,128)(2,1)S(1)} copy-done((bf16[1,128,512]{2,1,0:T(8,128)(2,1)S(1)}, bf16[1,128,512]{2,1,0:T(8,128)(2,1)}, u32[]{:S(2)}) %copy-start.2) | copy-done | bytes 131096
  4.1 0.0 copy-start.3
  4.1 0.9 %copy-done.3 = bf16[1,128,512]{2,1,0:T(8,128)(2,1)S(1)} copy-done((bf16[1,128,512]{2,1,0:T(8,128)(2,1)S(1)}, bf16[1,128,512]{2,1,0:T(8,128)(2,1)}, u32[]{:S(2)}) %copy-start.3) | copy-done | bytes 131096
  5.0 0.0 copy-start.4
  5.0 0.9 %copy-done.4 = bf16[128,512]{1,0:T(8,128)(2,1)S(1)} copy-done((bf16[128,512]{1,0:T(8,128)(2,1)S(1)}, bf16[128,512]{1,0:T(8,128)(2,1)}, u32[]{:S(2)}) %copy-start.4) | copy-done | bytes 131096
  5.9 0.0 copy-start.5
  5.9 0.9 %copy-done.5 = bf16[256,256]{1,0:T(8,128)(2,1)S(1)} copy-done((bf16[256,256]{1,0:T(8,128)(2,1)S(1)}, bf16[256,256]{1,0:T(8,128)(2,1)}, u32[]{:S(2)}) %copy-start.5) | copy-done | bytes 131096
  6.8 0.0 copy-start.6
  6.8 0.9 %copy-done.6 = bf16[256,256]{1,0:T(8,128)(2,1)S(1)} copy-done((bf16[256,256]{1,0:T(8,128)(2,1)S(1)}, bf16[256,256]{1,0:T(8,128)(2,1)}, u32[]{:S(2)}) %copy-start.6) | copy-done | bytes 131096
  7.7 0.0 copy-start.7
  7.7 0.8 %copy-done.7 = f32[2,64,128]{2,1,0:T(8,128)S(1)} copy-done((f32[2,64,128]{2,1,0:T(8,128)S(1)}, f32[2,64,128]{2,1,0:T(8,128)}, u32[]{:S(2)}) %copy-start.7) | copy-done | bytes 65560
  8.6 49.5 %exchange.1 = (bf16[128,512]{1,0:T(8,128)(2,1)S(1)}, bf16[128,512]{1,0:T(8,128)(2,1)S(1)}, bf16[128,512]{1,0:T(8,128)(2,1)S(1)}, bf16[128,512]{1,0:T(8,128)(2,1)...) custom-call(bf16[128,512]{1,0:T(8,128)(2,1)S(1)} %bitcast.6, ...), custom_call_target="tpu_custom_call" | custom-call | tf_op jit(solution)/shard_map/exchange/pallas_call | solution.py:318
  58.1 1.2 %finish.1 = (bf16[1,128,512]{2,1,0:T(8,128)(2,1)}, bf16[1,128,512]{2,1,0:T(8,128)(2,1)}, bf16[1,128,512]{2,1,0:T(8,128)(2,1)}, bf16[1,128,512]{2,1,0:T(8,128)(2,1)}, bf16[128,512]{1,0:T(8,128)(2,1)}) custom-call(bf16[128,512]{1,0:T(8,128)(2,1)S(1)} %get-tuple-element.12.conv_ref, bf16[128,512]{1,0:T(8,128)(2,1)S(1)} %get-tuple-element.13.back_ref, ...), custom_call_target="tpu_custom_call" | custom-call | tf_op jit(solution)/shard_map/finish/pallas_call | solution.py:363
Async XLA Ops:
  0.6 0.7 %copy-start.9 = (bf16[64,128]{1,0:T(8,128)(2,1)S(1)}, bf16[64,128]{1,0:T(8,128)(2,1)}, u32[]{:S(2)}) copy-start(bf16[64,128]{1,0:T(8,128)(2,1)} %constant.13.clone.last_ref) | copy-start | bytes 49156
  0.6 0.8 %copy-start.8 = (bf16[128,64]{1,0:T(8,128)(2,1)S(1)}, bf16[128,64]{1,0:T(8,128)(2,1)}, u32[]{:S(2)}) copy-start(bf16[128,64]{1,0:T(8,128)(2,1)} %constant.10.clone.first_ref) | copy-start | bytes 49156
  1.4 0.9 %copy-start = (bf16[1,128,512]{2,1,0:T(8,128)(2,1)S(1)}, bf16[1,128,512]{2,1,0:T(8,128)(2,1)}, u32[]{:S(2)}) copy-start(bf16[1,128,512]{2,1,0:T(8,128)(2,1)} %param.14) | copy-start | bytes 393220
  2.3 0.9 %copy-start.1 = (bf16[1,128,512]{2,1,0:T(8,128)(2,1)S(1)}, bf16[1,128,512]{2,1,0:T(8,128)(2,1)}, u32[]{:S(2)}) copy-start(bf16[1,128,512]{2,1,0:T(8,128)(2,1)} %param.11) | copy-start | bytes 393220
  3.2 0.9 %copy-start.2 = (bf16[1,128,512]{2,1,0:T(8,128)(2,1)S(1)}, bf16[1,128,512]{2,1,0:T(8,128)(2,1)}, u32[]{:S(2)}) copy-start(bf16[1,128,512]{2,1,0:T(8,128)(2,1)} %param.12) | copy-start | bytes 393220
  4.1 0.9 %copy-start.3 = (bf16[1,128,512]{2,1,0:T(8,128)(2,1)S(1)}, bf16[1,128,512]{2,1,0:T(8,128)(2,1)}, u32[]{:S(2)}) copy-start(bf16[1,128,512]{2,1,0:T(8,128)(2,1)} %param.13) | copy-start | bytes 393220
  5.0 0.9 %copy-start.4 = (bf16[128,512]{1,0:T(8,128)(2,1)S(1)}, bf16[128,512]{1,0:T(8,128)(2,1)}, u32[]{:S(2)}) copy-start(bf16[128,512]{1,0:T(8,128)(2,1)} %filt_ref.1) | copy-start | bytes 393220
  5.9 0.9 %copy-start.5 = (bf16[256,256]{1,0:T(8,128)(2,1)S(1)}, bf16[256,256]{1,0:T(8,128)(2,1)}, u32[]{:S(2)}) copy-start(bf16[256,256]{1,0:T(8,128)(2,1)} %constant.12.clone.back_middle_ref) | copy-start | bytes 393220
  6.8 0.9 %copy-start.6 = (bf16[256,256]{1,0:T(8,128)(2,1)S(1)}, bf16[256,256]{1,0:T(8,128)(2,1)}, u32[]{:S(2)}) copy-start(bf16[256,256]{1,0:T(8,128)(2,1)} %constant.11.clone.middle_ref) | copy-start | bytes 393220
  7.7 0.8 %copy-start.7 = (f32[2,64,128]{2,1,0:T(8,128)S(1)}, f32[2,64,128]{2,1,0:T(8,128)}, u32[]{:S(2)}) copy-start(f32[2,64,128]{2,1,0:T(8,128)} %constant.14.clone.twist_ref) | copy-start | bytes 196612

commit v2 on v1

--- a/solution.py
+++ b/solution.py
@@ -14,6 +14,7 @@
 MESH = pl.DeviceIdType.MESH
 F32 = jnp.float32
 BF16 = jnp.bfloat16
+GRANT = 54240 * 1024
 
 
 def tables(blocks, width):
@@ -29,14 +30,14 @@
     angle_pb = 2.0 * math.pi * (np.outer(p, p) % width) / width
     cos, sin = np.cos(angle_pb), np.sin(angle_pb)
     middle = np.block([[cos, -sin], [sin, cos]])
-    half = lambda x: jnp.asarray(x.astype(np.float32).astype(ml_dtypes.bfloat16))
-    return (
-        half(first),
-        half(middle),
-        half(middle.T),
-        half(last),
-        jnp.asarray(twist.astype(np.float32)),
-    )
+    half = np.zeros((2 * 2 * width + 2 * blocks + blocks, 2 * width), np.float32)
+    half[: 2 * width] = middle
+    half[2 * width : 4 * width] = middle.T
+    half[4 * width : 4 * width + 2 * blocks, :blocks] = first
+    half[4 * width + 2 * blocks :, : 2 * blocks] = last
+    wide = np.zeros((8 * blocks, width), np.float32)
+    wide[: 2 * blocks] = twist.reshape(2 * blocks, width)
+    return jnp.asarray(half.astype(ml_dtypes.bfloat16)), jnp.asarray(wide)
 
 
 def far_first(step, count):
@@ -46,24 +47,31 @@
 
 def main_kernel(
     sizes,
-    query_ref,
-    key_ref,
-    value_ref,
-    grad_ref,
-    feat_ref,
-    filt_ref,
-    first_ref,
-    middle_ref,
-    back_middle_ref,
-    last_ref,
-    twist_ref,
+    filt_hbm,
+    query_hbm,
+    key_hbm,
+    value_hbm,
+    grad_hbm,
+    feat_hbm,
+    table_hbm,
+    twist_hbm,
     conv_out,
     back_out,
     lag_out,
     qf_out,
     kf_out,
     vf_out,
+    grad_out,
     after_out,
+    taps,
+    filt_ref,
+    query_ref,
+    key_ref,
+    value_ref,
+    grad_ref,
+    feat_ref,
+    table_ref,
+    twist_ref,
     ext,
     rim_send,
     rim_recv,
@@ -86,11 +94,15 @@
     gate_spec,
     grad_spec,
     product,
+    load_sems,
     send_sems,
     recv_sems,
+    ring_sem,
 ):
     ctx, chans, fast = sizes
     tokens, width = query_ref.shape
+    middle_rows, back_rows = pl.ds(0, 2 * tokens), pl.ds(2 * tokens, 2 * tokens)
+    first_rows, last_rows = pl.ds(4 * tokens, 2 * ctx), pl.ds(4 * tokens + 2 * ctx, ctx)
     me = lax.axis_index("context")
     dp = lax.axis_index("dp")
     slow = ctx // fast
@@ -104,13 +116,44 @@
         s, f = far_first(step // fast, slow), far_first(lax.rem(step, fast), fast)
         return lax.rem(my_slow + s, slow) * fast + lax.rem(my_fast + f, fast)
 
-    @pl.loop(0, ctx - 1)
+    def tell(sem, device):
+        pl.semaphore_signal(sem, inc=1, device_id=device, device_id_type=MESH)
+
+    def in_slow_ring(step):
+        return lax.rem(my_slow + far_first(step, slow), slow) * fast + my_fast
+
+    def in_fast_ring(step):
+        return my_slow * fast + lax.rem(my_fast + far_first(step, fast), fast)
+
+    @pl.loop(0, slow - 1)
     def _(step):
-        pl.semaphore_signal(
-            barrier, inc=1, device_id={"context": peer_of(step)}, device_id_type=MESH
+        tell(barrier, {"context": in_slow_ring(step)})
+
+    @pl.loop(0, fast - 1)
+    def _(step):
+        tell(barrier, {"context": in_fast_ring(step)})
+
+    tell(barrier, {"context": following})
+    tell(barrier, {"context": previous})
+    tell(barrier, {"dp": partner})
+
+    loads = [
+        pltpu.make_async_copy(src, dst, load_sems.at[i])
+        for i, (src, dst) in enumerate(
+            (
+                (query_hbm, query_ref),
+                (key_hbm, key_ref),
+                (value_hbm, value_ref),
+                (feat_hbm, feat_ref),
+                (grad_hbm, grad_ref),
+                (filt_hbm, filt_ref),
+                (table_hbm, table_ref),
+                (twist_hbm.at[pl.ds(0, 2 * ctx)], twist_ref),
+            )
         )
-
-    pl.semaphore_signal(barrier, inc=1, device_id={"dp": partner}, device_id_type=MESH)
+    ]
+    for load in loads:
+        load.start()
 
     def remote(src, dst, which, device):
         return pltpu.make_async_remote_copy(
@@ -134,18 +177,25 @@
         rows = ref.at[pl.ds(0, ctx - 1)]
         pltpu.make_async_copy(rows, rows, sems.at[which]).wait()
 
-    filt_send[...] = filt_ref[...].astype(F32).T.reshape(ctx, chans, tokens).astype(BF16)
-    tail = pl.ds(tokens - 8, 8)
-    rim_send[0, 0:2] = query_ref[tokens - 16 :].astype(F32)[14:]
-    rim_send[0, 2:4] = key_ref[tokens - 16 :].astype(F32)[14:]
-    rim_send[0, 4:6] = value_ref[tokens - 16 :].astype(F32)[14:]
+    for load in loads[:3]:
+        load.wait()
+    for row, rows_ref in enumerate((query_ref, key_ref, value_ref)):
+        rim_send[0, 2 * row : 2 * row + 2] = rows_ref[tokens - 16 :].astype(F32)[14:]
     rim_send[0, 6:8] = jnp.zeros((2, width), F32)
 
-    pl.semaphore_wait(barrier, ctx)
+    pl.semaphore_wait(barrier, slow + fast + 1)
 
     rim_copy = remote(rim_send, rim_recv, 0, {"context": following})
     rim_copy.start()
-    scatter(filt_send, filt_recv, 1)
+
+    @pl.loop(0, slow - 1)
+    def _(step):
+        tell(ring_sem, {"context": in_slow_ring(step)})
+
+    for load in loads[3:]:
+        load.wait()
+    taps[...] = feat_ref[...].astype(F32)
+    filt_send[...] = filt_ref[...].astype(F32).T.reshape(ctx, chans, tokens).astype(BF16)
     rim_copy.wait()
 
     keep = jnp.where(me == 0, 0.0, 1.0).astype(F32)
@@ -155,7 +205,7 @@
         ext[6:8] = rim_recv[0, 2 * which : 2 * which + 2] * keep
         total = None
         for lag in range(3):
-            tap = feat_ref[which, lag : lag + 1, :]
+            tap = taps[which, lag : lag + 1, :]
             term = tap * ext[8 - lag : 8 - lag + tokens]
             total = term if total is None else total + term
         return total.astype(BF16)
@@ -166,25 +216,25 @@
     kf_out[...] = key_feat
     value_feat = featured(value_ref, 2)
     vf_out[...] = value_feat
+    grad_out[...] = grad_ref[...]
     gated = (key_feat.astype(F32) * value_feat.astype(F32)).T.reshape(ctx, chans, tokens)
     signal = (grad_ref[...].astype(F32) * query_feat.astype(F32)).T.reshape(ctx, chans, tokens)
     pair_send[...] = jnp.concatenate([gated, signal], axis=1).astype(BF16)
+    pl.semaphore_wait(ring_sem, slow - 1)
     scatter(pair_send, pair_recv, 2)
+    scatter(filt_send, filt_recv, 1)
 
     def spectra(wide_ref, rows, start, dest):
         for channel in range(chans):
             grid = wide_ref[pl.ds(start + channel, ctx, stride=rows), :].astype(BF16)
-            section = jnp.dot(first_ref[...], grid, preferred_element_type=F32)
+            section = jnp.dot(table_ref[first_rows, 0:ctx], grid, preferred_element_type=F32)
             real, imag = section[:ctx], section[ctx:]
-            cos, sin = twist_ref[0], twist_ref[1]
+            cos, sin = twist_ref[0:ctx], twist_ref[ctx : 2 * ctx]
             here = pl.ds(channel * ctx, ctx)
             turned[here, 0:tokens] = (real * cos + imag * sin).astype(BF16)
             turned[here, tokens : 2 * tokens] = (imag * cos - real * sin).astype(BF16)
-        dest[...] = jnp.dot(turned[...], middle_ref[...], preferred_element_type=F32)
-
-    wait_scatter(filt_recv, recv_sems, 1)
-    wide_filt[...] = filt_recv[...].astype(F32).reshape(ctx * chans, tokens)
-    spectra(wide_filt, chans, 0, filt_spec)
+        dest[...] = jnp.dot(turned[...], table_ref[middle_rows], preferred_element_type=F32)
+
     wait_scatter(pair_recv, recv_sems, 2)
     wide[...] = pair_recv[...].astype(F32).reshape(ctx * 2 * chans, tokens)
     spectra(wide, 2 * chans, 0, gate_spec)
@@ -196,14 +246,14 @@
     def inverse(real, imag, wide_ref, rows, start):
         product[:, 0:tokens] = real.astype(BF16)
         product[:, tokens : 2 * tokens] = imag.astype(BF16)
-        gate = jnp.dot(product[...], back_middle_ref[...], preferred_element_type=F32)
-        cos, sin = twist_ref[0], twist_ref[1]
+        gate = jnp.dot(product[...], table_ref[back_rows], preferred_element_type=F32)
+        cos, sin = twist_ref[0:ctx], twist_ref[ctx : 2 * ctx]
         for channel in range(chans):
             piece = gate[channel * ctx : (channel + 1) * ctx]
             real, imag = piece[:, :tokens], piece[:, tokens:]
             stacked = jnp.concatenate([real * cos - imag * sin, imag * cos + real * sin], axis=0)
             wide_ref[pl.ds(start + channel, ctx, stride=rows), :] = jnp.dot(
-                last_ref[...], stacked.astype(BF16), preferred_element_type=F32
+                table_ref[last_rows, 0 : 2 * ctx], stacked.astype(BF16), preferred_element_type=F32
             )
 
     gate_real, gate_imag = parts(gate_spec)
@@ -218,6 +268,9 @@
     part_send[...] = wide_filt[...].reshape(ctx, chans, tokens).astype(BF16)
     part_copy = remote(part_send, part_recv, 3, {"dp": partner})
     part_copy.start()
+    wait_scatter(filt_recv, recv_sems, 1)
+    wide_filt[...] = filt_recv[...].astype(F32).reshape(ctx * chans, tokens)
+    spectra(wide_filt, chans, 0, filt_spec)
     filt_real, filt_imag = parts(filt_spec)
     gate_real, gate_imag = parts(gate_spec)
     inverse(
@@ -278,7 +331,7 @@
     kf_ref,
     vf_ref,
     after_ref,
-    feat_ref,
+    taps_ref,
     out_ref,
     gq_ref,
     gk_ref,
@@ -296,7 +349,7 @@
         ext[tokens : tokens + 2] = after_ref[2 * which : 2 * which + 2]
         total = None
         for lag in range(3):
-            term = feat_ref[which, lag : lag + 1, :] * ext[lag : lag + tokens]
+            term = taps_ref[which, lag : lag + 1, :] * ext[lag : lag + tokens]
             total = term if total is None else total + term
         dest[0] = total.astype(BF16)
 
@@ -309,9 +362,18 @@
 def on_device(ctx, queries, key_gates, values, out_grad, featurizer, long_filter):
     tokens, width = long_filter.shape
     chans = width // ctx
-    fast = 8
-    consts = tables(ctx, tokens)
-    taps = featurizer.astype(F32)
+    fast = 1 << ((ctx.bit_length() - 1) // 2)
+    table, twist = tables(ctx, tokens)
+    operands = (
+        long_filter,
+        queries[0],
+        key_gates[0],
+        values[0],
+        out_grad[0],
+        featurizer,
+        table,
+        twist,
+    )
     vmem = pl.BlockSpec(memory_space=pltpu.VMEM)
     like = lambda *shape, dtype=BF16: jax.ShapeDtypeStruct(shape, dtype)
     buf = lambda *shape, dtype=BF16: pltpu.VMEM(shape, dtype)
@@ -324,11 +386,15 @@
             like(tokens, width),
             like(tokens, width),
             like(tokens, width),
+            like(tokens, width),
             like(8, width, dtype=F32),
+            like(*featurizer.shape, dtype=F32),
         ),
-        in_specs=[vmem] * 11,
-        out_specs=(vmem,) * 7,
+        in_specs=[pl.BlockSpec(memory_space=pltpu.HBM)] * len(operands),
+        out_specs=(vmem,) * 9,
         scratch_shapes=[
+            *(buf(*x.shape, dtype=x.dtype) for x in operands[:-1]),
+            buf(2 * ctx, tokens, dtype=F32),
             buf(tokens + 16, width, dtype=F32),
             buf(1, 8, width, dtype=F32),
             buf(1, 8, width, dtype=F32),
@@ -351,15 +417,17 @@
             buf(ctx * chans, 2 * tokens, dtype=F32),
             buf(ctx * chans, 2 * tokens, dtype=F32),
             buf(ctx * chans, 2 * tokens),
+            pltpu.SemaphoreType.DMA((len(operands),)),
             pltpu.SemaphoreType.DMA((7,)),
             pltpu.SemaphoreType.DMA((7,)),
+            pltpu.SemaphoreType.REGULAR,
         ],
         compiler_params=pltpu.CompilerParams(
-            collective_id=0, has_side_effects=True, vmem_limit_bytes=48 * 1024 * 1024
+            collective_id=0, has_side_effects=True, vmem_limit_bytes=GRANT
         ),
         name="exchange",
-    )(queries[0], key_gates[0], values[0], out_grad[0], taps, long_filter, *consts)
-    conv, back, lag, qf, kf, vf, after = results
+    )(*operands)
+    conv, back, lag, qf, kf, vf, grad, after, taps = results
     return pl.pallas_call(
         final_kernel,
         out_shape=(like(1, tokens, width),) * 4 + (like(tokens, width),),
@@ -368,7 +436,7 @@
         scratch_shapes=[buf(tokens + 16, width, dtype=F32)],
         compiler_params=pltpu.CompilerParams(vmem_limit_bytes=32 * 1024 * 1024),
         name="finish",
-    )(conv, back, lag, out_grad[0], qf, kf, vf, after, taps)
+    )(conv, back, lag, grad, qf, kf, vf, after, taps)
 
 
 def solution(mesh):

time: 59.7 us -> 52.8 us (0.88)
  local copies, waits for them, and re-layouts: 7.21 us -> 0.7 us
  other arithmetic: 0.72 us -> 0 us
    unnamed x20 -> x2, local copies, waits for them, and re-layouts: 7.21 us -> 0.7 us
    convert_element_type x1 -> x0, other arithmetic: 0.72 us -> none  [on_device(): taps = featurizer.astype(F32)]
where the time goes in v2:
time: 52.8 us; the launch traced here: 52.6 us
  Pallas kernels  51.2 us (97%)
  local copies, waits for them, and re-layouts  0.7 us (1%)
  between operations  0.65 us (1%)
    pallas_call x1, Pallas kernels, on_device(): pl.pallas_call(functools.partial(main_kernel, (ctx, chans, fast)), out_sh...  50 us
    pallas_call x1, Pallas kernels, on_device(): pl.pallas_call(final_kernel, out_shape=(like(1, tokens, width),) * 4 + (l...  1.24 us

profile of v2, /device:TPU:112, one launch (start us, length us, event | category | flops | bytes accessed | tf_op | source)
XLA Modules:
  0.0 52.6 jit_solution(9820189720158588416)
XLA Ops:
  0.6 0.0 copy-start
  0.6 0.7 %copy-done = bf16[3,3,512]{2,1,0:T(4,128)(2,1)S(1)} copy-done((bf16[3,3,512]{2,1,0:T(4,128)(2,1)S(1)}, bf16[3,3,512]{2,1,0:T(4,128)(2,1)}, u32[]{:S(2)}) %copy-start) | copy-done | bytes 9240
  1.3 50.0 %exchange.1 = (bf16[128,512]{1,0:T(8,128)(2,1)S(1)}, bf16[128,512]{1,0:T(8,128)(2,1)S(1)}, bf16[128,512]{1,0:T(8,128)(2,1)S(1)}, bf16[128,512]{1,0:T(8,128)(2,1)...) custom-call(bf16[128,512]{1,0:T(8,128)(2,1)} %filt_hbm.1, ...), custom_call_target="tpu_custom_call" | custom-call | tf_op jit(solution)/shard_map/exchange/pallas_call | solution.py:380
  51.3 1.2 %finish.1 = (bf16[1,128,512]{2,1,0:T(8,128)(2,1)}, bf16[1,128,512]{2,1,0:T(8,128)(2,1)}, bf16[1,128,512]{2,1,0:T(8,128)(2,1)}, bf16[1,128,512]{2,1,0:T(8,128)(2,1)}, bf16[128,512]{1,0:T(8,128)(2,1)}) custom-call(bf16[128,512]{1,0:T(8,128)(2,1)S(1)} %get-tuple-element.14.conv_ref, bf16[128,512]{1,0:T(8,128)(2,1)S(1)} %get-tuple-element.15.back_ref, ...), custom_call_target="tpu_custom_call" | custom-call | tf_op jit(solution)/shard_map/finish/pallas_call | solution.py:431
Async XLA Ops:
  0.6 0.7 %copy-start = (bf16[3,3,512]{2,1,0:T(4,128)(2,1)S(1)}, bf16[3,3,512]{2,1,0:T(4,128)(2,1)}, u32[]{:S(2)}) copy-start(bf16[3,3,512]{2,1,0:T(4,128)(2,1)} %feat_hbm.1) | copy-start | bytes 27652

commit v3 on v2

--- a/solution.py
+++ b/solution.py
@@ -78,10 +78,10 @@
     after_send,
     after_recv,
     filt_send,
+    filt_mid,
     filt_recv,
     pair_send,
     pair_recv,
-    part_send,
     part_recv,
     conv_send,
     conv_recv,
@@ -173,8 +173,16 @@
 
         dst[me] = src[me]
 
+    def ring_scatter(src, dst, place, mine, count, which):
+        @pl.loop(0, count - 1)
+        def _(step):
+            at = lax.rem(mine + far_first(step, count), count)
+            remote(src.at[:, at], dst.at[mine], which, {"context": place(step)}).start()
+
+        dst[mine] = src[:, mine]
+
     def wait_scatter(ref, sems, which):
-        rows = ref.at[pl.ds(0, ctx - 1)]
+        rows = ref.at[pl.ds(0, ref.shape[0] - 1)]
         pltpu.make_async_copy(rows, rows, sems.at[which]).wait()
 
     for load in loads[:3]:
@@ -183,6 +191,12 @@
         rim_send[0, 2 * row : 2 * row + 2] = rows_ref[tokens - 16 :].astype(F32)[14:]
     rim_send[0, 6:8] = jnp.zeros((2, width), F32)
 
+    for load in loads[3:]:
+        load.wait()
+    taps[...] = feat_ref[...].astype(F32)
+    by_channel = filt_ref[...].astype(F32).T.reshape(slow, fast, chans, tokens)
+    filt_send[...] = by_channel.astype(BF16)
+
     pl.semaphore_wait(barrier, slow + fast + 1)
 
     rim_copy = remote(rim_send, rim_recv, 0, {"context": following})
@@ -192,10 +206,7 @@
     def _(step):
         tell(ring_sem, {"context": in_slow_ring(step)})
 
-    for load in loads[3:]:
-        load.wait()
-    taps[...] = feat_ref[...].astype(F32)
-    filt_send[...] = filt_ref[...].astype(F32).T.reshape(ctx, chans, tokens).astype(BF16)
+    ring_scatter(filt_send, filt_mid, in_fast_ring, my_fast, fast, 1)
     rim_copy.wait()
 
     keep = jnp.where(me == 0, 0.0, 1.0).astype(F32)
@@ -222,7 +233,8 @@
     pair_send[...] = jnp.concatenate([gated, signal], axis=1).astype(BF16)
     pl.semaphore_wait(ring_sem, slow - 1)
     scatter(pair_send, pair_recv, 2)
-    scatter(filt_send, filt_recv, 1)
+    wait_scatter(filt_mid, recv_sems, 1)
+    ring_scatter(filt_mid, filt_recv, in_slow_ring, my_slow, slow, 7)
 
     def spectra(wide_ref, rows, start, dest):
         for channel in range(chans):
@@ -265,10 +277,9 @@
         chans,
         0,
     )
-    part_send[...] = wide_filt[...].reshape(ctx, chans, tokens).astype(BF16)
-    part_copy = remote(part_send, part_recv, 3, {"dp": partner})
-    part_copy.start()
-    wait_scatter(filt_recv, recv_sems, 1)
+    lag_send[...] = wide_filt[...].reshape(ctx, chans, tokens).astype(BF16)
+    scatter(lag_send, lag_recv, 5)
+    wait_scatter(filt_recv, recv_sems, 7)
     wide_filt[...] = filt_recv[...].astype(F32).reshape(ctx * chans, tokens)
     spectra(wide_filt, chans, 0, filt_spec)
     filt_real, filt_imag = parts(filt_spec)
@@ -291,9 +302,9 @@
     )
     conv_send[...] = wide[...].reshape(ctx, 2 * chans, tokens).astype(BF16)
     scatter(conv_send, conv_recv, 4)
-    part_copy.wait()
-    lag_send[...] = (part_send[...].astype(F32) + part_recv[...].astype(F32)).astype(BF16)
-    scatter(lag_send, lag_recv, 5)
+    wait_scatter(lag_recv, recv_sems, 5)
+    part_copy = remote(lag_recv, part_recv, 3, {"dp": partner})
+    part_copy.start()
 
     wait_scatter(conv_recv, recv_sems, 4)
     both = conv_recv[...].astype(F32)
@@ -312,11 +323,13 @@
     after_send[0, 6:8] = jnp.zeros((2, width), F32)
     after_copy = remote(after_send, after_recv, 6, {"context": previous})
     after_copy.start()
-    wait_scatter(lag_recv, recv_sems, 5)
-    lag_out[...] = lag_recv[...].astype(F32).reshape(width, tokens).T.astype(BF16)
+    part_copy.wait()
+    lag_sum = lag_recv[...].astype(F32) + part_recv[...].astype(F32)
+    lag_out[...] = lag_sum.reshape(width, tokens).T.astype(BF16)
     after_copy.wait()
     after_out[...] = after_recv[0] * jnp.where(me == ctx - 1, 0.0, 1.0).astype(F32)
-    wait_scatter(filt_send, send_sems, 1)
+    wait_scatter(filt_mid, send_sems, 1)
+    wait_scatter(filt_recv, send_sems, 7)
     wait_scatter(pair_send, send_sems, 2)
     wait_scatter(conv_send, send_sems, 4)
     wait_scatter(lag_send, send_sems, 5)
@@ -364,6 +377,7 @@
     chans = width // ctx
     fast = 1 << ((ctx.bit_length() - 1) // 2)
     table, twist = tables(ctx, tokens)
+    slow = ctx // fast
     operands = (
         long_filter,
         queries[0],
@@ -400,11 +414,11 @@
             buf(1, 8, width, dtype=F32),
             buf(1, 8, width, dtype=F32),
             buf(1, 8, width, dtype=F32),
-            buf(ctx, chans, tokens),
-            buf(ctx, chans, tokens),
+            buf(slow, fast, chans, tokens),
+            buf(fast, slow, chans, tokens),
+            buf(slow, fast, chans, tokens),
             buf(ctx, 2 * chans, tokens),
             buf(ctx, 2 * chans, tokens),
-            buf(ctx, chans, tokens),
             buf(ctx, chans, tokens),
             buf(ctx, 2 * chans, tokens),
             buf(ctx, 2 * chans, tokens),
@@ -418,8 +432,8 @@
             buf(ctx * chans, 2 * tokens, dtype=F32),
             buf(ctx * chans, 2 * tokens),
             pltpu.SemaphoreType.DMA((len(operands),)),
-            pltpu.SemaphoreType.DMA((7,)),
-            pltpu.SemaphoreType.DMA((7,)),
+            pltpu.SemaphoreType.DMA((8,)),
+            pltpu.SemaphoreType.DMA((8,)),
             pltpu.SemaphoreType.REGULAR,
         ],
         compiler_params=pltpu.CompilerParams(

time: 52.8 us -> 51.8 us (0.981)
  Pallas kernels: 51.2 us -> 50 us
    pallas_call x1, Pallas kernels: 50 us -> 48.8 us  [on_device(): pl.pallas_call(functools.partial(main_kernel, (ctx, chans, fast)), out_sh...]
where the time goes in v3:
time: 51.8 us; the launch traced here: 51.3 us
  Pallas kernels  50 us (97%)
  local copies, waits for them, and re-layouts  0.7 us (1%)
  between operations  0.65 us (1%)
    pallas_call x1, Pallas kernels, on_device(): pl.pallas_call(functools.partial(main_kernel, (ctx, chans, fast)), out_sh...  48.8 us
    pallas_call x1, Pallas kernels, on_device(): pl.pallas_call(final_kernel, out_shape=(like(1, tokens, width),) * 4 + (l...  1.24 us

profile of v3, /device:TPU:112, one launch (start us, length us, event | category | flops | bytes accessed | tf_op | source)
XLA Modules:
  0.0 51.3 jit_solution(14005398706822768522)
XLA Ops:
  0.6 0.0 copy-start
  0.6 0.7 %copy-done = bf16[3,3,512]{2,1,0:T(4,128)(2,1)S(1)} copy-done((bf16[3,3,512]{2,1,0:T(4,128)(2,1)S(1)}, bf16[3,3,512]{2,1,0:T(4,128)(2,1)}, u32[]{:S(2)}) %copy-start) | copy-done | bytes 9240
  1.3 48.8 %exchange.1 = (bf16[128,512]{1,0:T(8,128)(2,1)S(1)}, bf16[128,512]{1,0:T(8,128)(2,1)S(1)}, bf16[128,512]{1,0:T(8,128)(2,1)S(1)}, bf16[128,512]{1,0:T(8,128)(2,1)...) custom-call(bf16[128,512]{1,0:T(8,128)(2,1)} %filt_hbm.1, ...), custom_call_target="tpu_custom_call" | custom-call | tf_op jit(solution)/shard_map/exchange/pallas_call | solution.py:394
  50.1 1.2 %finish.1 = (bf16[1,128,512]{2,1,0:T(8,128)(2,1)}, bf16[1,128,512]{2,1,0:T(8,128)(2,1)}, bf16[1,128,512]{2,1,0:T(8,128)(2,1)}, bf16[1,128,512]{2,1,0:T(8,128)(2,1)}, bf16[128,512]{1,0:T(8,128)(2,1)}) custom-call(bf16[128,512]{1,0:T(8,128)(2,1)S(1)} %get-tuple-element.14.conv_ref, bf16[128,512]{1,0:T(8,128)(2,1)S(1)} %get-tuple-element.15.back_ref, ...), custom_call_target="tpu_custom_call" | custom-call | tf_op jit(solution)/shard_map/finish/pallas_call | solution.py:445
Async XLA Ops:
  0.6 0.7 %copy-start = (bf16[3,3,512]{2,1,0:T(4,128)(2,1)S(1)}, bf16[3,3,512]{2,1,0:T(4,128)(2,1)}, u32[]{:S(2)}) copy-start(bf16[3,3,512]{2,1,0:T(4,128)(2,1)} %feat_hbm.1) | copy-start | bytes 27652

commit v4 on v3

--- a/solution.py
+++ b/solution.py
@@ -14,7 +14,7 @@
 MESH = pl.DeviceIdType.MESH
 F32 = jnp.float32
 BF16 = jnp.bfloat16
-GRANT = 54240 * 1024
+GRANT = 40000 * 1024
 
 
 def tables(blocks, width):
@@ -75,8 +75,11 @@
     ext,
     rim_send,
     rim_recv,
-    after_send,
-    after_recv,
+    head_send,
+    head_recv,
+    feat_next,
+    heads_send,
+    heads_recv,
     filt_send,
     filt_mid,
     filt_recv,
@@ -165,13 +168,18 @@
             device_id_type=MESH,
         )
 
-    def scatter(src, dst, which):
+    def scatter(src, dst, which, with_heads=False):
         @pl.loop(0, ctx - 1)
         def _(step):
             peer = peer_of(step)
             remote(src.at[peer], dst.at[me], which, {"context": peer}).start()
+            if with_heads:
+                after = lax.rem(peer + 1, ctx)
+                remote(heads_send.at[after], heads_recv.at[me], 8, {"context": peer}).start()
 
         dst[me] = src[me]
+        if with_heads:
+            heads_recv[me] = heads_send[following]
 
     def ring_scatter(src, dst, place, mine, count, which):
         @pl.loop(0, count - 1)
@@ -194,6 +202,9 @@
     for load in loads[3:]:
         load.wait()
     taps[...] = feat_ref[...].astype(F32)
+    for row, rows_ref in enumerate((grad_ref, key_ref, value_ref)):
+        head_send[0, 2 * row : 2 * row + 2] = rows_ref[:16].astype(F32)[:2]
+    head_send[0, 6:8] = jnp.zeros((2, width), F32)
     by_channel = filt_ref[...].astype(F32).T.reshape(slow, fast, chans, tokens)
     filt_send[...] = by_channel.astype(BF16)
 
@@ -201,6 +212,8 @@
 
     rim_copy = remote(rim_send, rim_recv, 0, {"context": following})
     rim_copy.start()
+    head_copy = remote(head_send, head_recv, 6, {"context": previous})
+    head_copy.start()
 
     @pl.loop(0, slow - 1)
     def _(step):
@@ -208,24 +221,33 @@
 
     ring_scatter(filt_send, filt_mid, in_fast_ring, my_fast, fast, 1)
     rim_copy.wait()
+    head_copy.wait()
 
     keep = jnp.where(me == 0, 0.0, 1.0).astype(F32)
 
-    def featured(rows_ref, which):
-        ext[8 : 8 + tokens] = rows_ref[...].astype(F32)
-        ext[6:8] = rim_recv[0, 2 * which : 2 * which + 2] * keep
+    def featured(rows_ref, which, start=8, count=None):
+        if count is None:
+            count = tokens
+            ext[8 : 8 + tokens] = rows_ref[...].astype(F32)
+            ext[6:8] = rim_recv[0, 2 * which : 2 * which + 2] * keep
         total = None
         for lag in range(3):
             tap = taps[which, lag : lag + 1, :]
-            term = tap * ext[8 - lag : 8 - lag + tokens]
+            term = tap * ext[start - lag : start - lag + count]
             total = term if total is None else total + term
         return total.astype(BF16)
+
+    def featured_after(which):
+        ext[8 + tokens : 10 + tokens] = head_recv[0, 2 * which : 2 * which + 2]
+        return featured(None, which, 8 + tokens, 2).astype(F32)
 
     query_feat = featured(query_ref, 0)
     qf_out[...] = query_feat
     key_feat = featured(key_ref, 1)
+    feat_next[0:2] = featured_after(1)
     kf_out[...] = key_feat
     value_feat = featured(value_ref, 2)
+    feat_next[2:4] = featured_after(2)
     vf_out[...] = value_feat
     grad_out[...] = grad_ref[...]
     gated = (key_feat.astype(F32) * value_feat.astype(F32)).T.reshape(ctx, chans, tokens)
@@ -255,7 +277,9 @@
     def parts(ref):
         return ref[:, 0:tokens], ref[:, tokens : 2 * tokens]
 
-    def inverse(real, imag, wide_ref, rows, start):
+    lane = lax.broadcasted_iota(jnp.int32, (ctx, tokens), 1)
+
+    def inverse(real, imag, wide_ref, rows, start, heads=None):
         product[:, 0:tokens] = real.astype(BF16)
         product[:, tokens : 2 * tokens] = imag.astype(BF16)
         gate = jnp.dot(product[...], table_ref[back_rows], preferred_element_type=F32)
@@ -264,9 +288,13 @@
             piece = gate[channel * ctx : (channel + 1) * ctx]
             real, imag = piece[:, :tokens], piece[:, tokens:]
             stacked = jnp.concatenate([real * cos - imag * sin, imag * cos + real * sin], axis=0)
-            wide_ref[pl.ds(start + channel, ctx, stride=rows), :] = jnp.dot(
+            result = jnp.dot(
                 table_ref[last_rows, 0 : 2 * ctx], stacked.astype(BF16), preferred_element_type=F32
             )
+            wide_ref[pl.ds(start + channel, ctx, stride=rows), :] = result
+            if heads is not None:
+                head = jnp.where(lane < 2, result, 0.0)
+                heads.append(pltpu.roll(head, 2 * (start + channel), 1))
 
     gate_real, gate_imag = parts(gate_spec)
     grad_real, grad_imag = parts(grad_spec)
@@ -280,6 +308,7 @@
     lag_send[...] = wide_filt[...].reshape(ctx, chans, tokens).astype(BF16)
     scatter(lag_send, lag_recv, 5)
     wait_scatter(filt_recv, recv_sems, 7)
+    heads = []
     wide_filt[...] = filt_recv[...].astype(F32).reshape(ctx * chans, tokens)
     spectra(wide_filt, chans, 0, filt_spec)
     filt_real, filt_imag = parts(filt_spec)
@@ -290,6 +319,7 @@
         wide,
         2 * chans,
         0,
+        heads,
     )
     filt_real, filt_imag = parts(filt_spec)
     grad_real, grad_imag = parts(grad_spec)
@@ -299,9 +329,11 @@
         wide,
         2 * chans,
         chans,
-    )
+        heads,
+    )
+    heads_send[...] = sum(heads).reshape(ctx, 1, tokens)
     conv_send[...] = wide[...].reshape(ctx, 2 * chans, tokens).astype(BF16)
-    scatter(conv_send, conv_recv, 4)
+    scatter(conv_send, conv_recv, 4, True)
     wait_scatter(lag_recv, recv_sems, 5)
     part_copy = remote(lag_recv, part_recv, 3, {"dp": partner})
     part_copy.start()
@@ -316,18 +348,32 @@
     def rounded(x):
         return x.astype(BF16).astype(F32)
 
-    head = 16
-    after_send[0, 0:2] = rounded(grad_ref[:head].astype(F32) * conv[:head])[:2]
-    after_send[0, 2:4] = rounded(vf_out[:head].astype(F32) * back[:head])[:2]
-    after_send[0, 4:6] = rounded(kf_out[:head].astype(F32) * back[:head])[:2]
-    after_send[0, 6:8] = jnp.zeros((2, width), F32)
-    after_copy = remote(after_send, after_recv, 6, {"context": previous})
-    after_copy.start()
+    wait_scatter(heads_recv, recv_sems, 8)
+    packed = heads_recv[...].reshape(ctx, tokens).astype(BF16)
+    from_lane = lax.broadcasted_iota(jnp.int32, (tokens, width), 0)
+    to_chan = lax.broadcasted_iota(jnp.int32, (tokens, width), 1) % chans
+    holder = lax.broadcasted_iota(jnp.int32, (ctx, width), 0)
+    is_mine = lax.broadcasted_iota(jnp.int32, (ctx, width), 1) // chans == holder
+
+    def next_row(kind, position):
+        pick = from_lane == 2 * (to_chan + chans * kind) + position
+        spread = jnp.dot(packed, jnp.where(pick, 1.0, 0.0).astype(BF16), preferred_element_type=F32)
+        return jnp.sum(jnp.where(is_mine, spread, 0.0), axis=0, keepdims=True)
+
+    last_keep = jnp.where(me == ctx - 1, 0.0, 1.0).astype(F32)
+    for position in range(2):
+        conv_next, back_next = next_row(0, position), next_row(1, position)
+        at = slice(position, position + 1)
+        after_out[at] = rounded(head_recv[0, at] * conv_next) * last_keep
+        at = slice(2 + position, 3 + position)
+        after_out[at] = rounded(feat_next[at] * back_next) * last_keep
+        into = slice(4 + position, 5 + position)
+        after_out[into] = rounded(feat_next[slice(position, position + 1)] * back_next) * last_keep
+    after_out[6:8] = jnp.zeros((2, width), F32)
     part_copy.wait()
     lag_sum = lag_recv[...].astype(F32) + part_recv[...].astype(F32)
     lag_out[...] = lag_sum.reshape(width, tokens).T.astype(BF16)
-    after_copy.wait()
-    after_out[...] = after_recv[0] * jnp.where(me == ctx - 1, 0.0, 1.0).astype(F32)
+    wait_scatter(heads_send, send_sems, 8)
     wait_scatter(filt_mid, send_sems, 1)
     wait_scatter(filt_recv, send_sems, 7)
     wait_scatter(pair_send, send_sems, 2)
@@ -414,6 +460,9 @@
             buf(1, 8, width, dtype=F32),
             buf(1, 8, width, dtype=F32),
             buf(1, 8, width, dtype=F32),
+            buf(8, width, dtype=F32),
+            buf(ctx, 1, tokens, dtype=F32),
+            buf(ctx, 1, tokens, dtype=F32),
             buf(slow, fast, chans, tokens),
             buf(fast, slow, chans, tokens),
             buf(slow, fast, chans, tokens),
@@ -432,15 +481,15 @@
             buf(ctx * chans, 2 * tokens, dtype=F32),
             buf(ctx * chans, 2 * tokens),
             pltpu.SemaphoreType.DMA((len(operands),)),
-            pltpu.SemaphoreType.DMA((8,)),
-            pltpu.SemaphoreType.DMA((8,)),
+            pltpu.SemaphoreType.DMA((9,)),
+            pltpu.SemaphoreType.DMA((9,)),
             pltpu.SemaphoreType.REGULAR,
         ],
         compiler_params=pltpu.CompilerParams(
             collective_id=0, has_side_effects=True, vmem_limit_bytes=GRANT
         ),
         name="exchange",
-    )(*operands)
+    )(*(pltpu.with_memory_space_constraint(x, pltpu.HBM) for x in operands))
     conv, back, lag, qf, kf, vf, grad, after, taps = results
     return pl.pallas_call(
         final_kernel,

time: 51.8 us -> 49.7 us (0.959)
  the two profiles are of different devices: /device:TPU:112 before, /device:TPU:1 now
where the time goes in v4:
time: 49.7 us; the launch traced here: 49.5 us
  Pallas kernels  48.9 us (98%)
  between operations  0.64 us (1%)
    pallas_call x1, Pallas kernels, on_device(): pl.pallas_call(functools.partial(main_kernel, (ctx, chans, fast)), out_sh...  47.6 us
    pallas_call x1, Pallas kernels, on_device(): pl.pallas_call(final_kernel, out_shape=(like(1, tokens, width),) * 4 + (l...  1.23 us

profile of v4, /device:TPU:1, one launch (start us, length us, event | category | flops | bytes accessed | tf_op | source)
XLA Modules:
  0.0 49.5 jit_solution(3098617684891508709)
XLA Ops:
  0.6 47.6 %exchange.1 = (bf16[128,512]{1,0:T(8,128)(2,1)S(1)}, bf16[128,512]{1,0:T(8,128)(2,1)S(1)}, bf16[128,512]{1,0:T(8,128)(2,1)S(1)}, bf16[128,512]{1,0:T(8,128)(2,1)...) custom-call(bf16[128,512]{1,0:T(8,128)(2,1)} %filt_hbm.1, ...), custom_call_target="tpu_custom_call" | custom-call | tf_op jit(solution)/shard_map/exchange/pallas_call | solution.py:440
  48.3 1.2 %finish.1 = (bf16[1,128,512]{2,1,0:T(8,128)(2,1)}, bf16[1,128,512]{2,1,0:T(8,128)(2,1)}, bf16[1,128,512]{2,1,0:T(8,128)(2,1)}, bf16[1,128,512]{2,1,0:T(8,128)(2,1)}, bf16[128,512]{1,0:T(8,128)(2,1)}) custom-call(bf16[128,512]{1,0:T(8,128)(2,1)S(1)} %get-tuple-element.14.conv_ref, bf16[128,512]{1,0:T(8,128)(2,1)S(1)} %get-tuple-element.15.back_ref, ...), custom_call_target="tpu_custom_call" | custom-call | tf_op jit(solution)/shard_map/finish/pallas_call | solution.py:494

commit v5 on v4

--- a/solution.py
+++ b/solution.py
@@ -43,6 +43,10 @@
 def far_first(step, count):
     up = (step + 1) // 2
     return lax.rem(count // 2 + jnp.where(lax.rem(step, 2) == 1, up, count - step // 2), count)
+
+
+def far_offsets(count):
+    return [(count // 2 + ((i + 1) // 2 if i % 2 else -(i // 2))) % count for i in range(count)]
 
 
 def main_kernel(
@@ -115,10 +119,6 @@
 
     barrier = pltpu.get_barrier_semaphore()
 
-    def peer_of(step):
-        s, f = far_first(step // fast, slow), far_first(lax.rem(step, fast), fast)
-        return lax.rem(my_slow + s, slow) * fast + lax.rem(my_fast + f, fast)
-
     def tell(sem, device):
         pl.semaphore_signal(sem, inc=1, device_id=device, device_id_type=MESH)
 
@@ -168,18 +168,25 @@
             device_id_type=MESH,
         )
 
+    fast_places = [lax.rem(my_fast + offset, fast) for offset in far_offsets(fast)]
+
     def scatter(src, dst, which, with_heads=False):
-        @pl.loop(0, ctx - 1)
+        def send_row(row, count):
+            base = row * fast
+            for place in fast_places[:count]:
+                peer = base + place
+                remote(src.at[peer], dst.at[me], which, {"context": peer}).start()
+                if with_heads:
+                    remote(heads_send.at[peer], heads_recv.at[me], 8, {"context": peer}).start()
+
+        @pl.loop(0, slow - 1)
         def _(step):
-            peer = peer_of(step)
-            remote(src.at[peer], dst.at[me], which, {"context": peer}).start()
-            if with_heads:
-                after = lax.rem(peer + 1, ctx)
-                remote(heads_send.at[after], heads_recv.at[me], 8, {"context": peer}).start()
-
+            send_row(lax.rem(my_slow + far_first(step, slow), slow), fast)
+
+        send_row(my_slow, fast - 1)
         dst[me] = src[me]
         if with_heads:
-            heads_recv[me] = heads_send[following]
+            heads_recv[me] = heads_send[me]
 
     def ring_scatter(src, dst, place, mine, count, which):
         @pl.loop(0, count - 1)
@@ -331,7 +338,7 @@
         chans,
         heads,
     )
-    heads_send[...] = sum(heads).reshape(ctx, 1, tokens)
+    heads_send[...] = pltpu.roll(sum(heads), ctx - 1, 0).reshape(ctx, 1, tokens)
     conv_send[...] = wide[...].reshape(ctx, 2 * chans, tokens).astype(BF16)
     scatter(conv_send, conv_recv, 4, True)
     wait_scatter(lag_recv, recv_sems, 5)

time: 49.7 us -> 49.2 us (0.990)
  the two profiles are of different devices: /device:TPU:1 before, /device:TPU:38 now
where the time goes in v5:
time: 49.2 us; the launch traced here: 49 us
  Pallas kernels  48.3 us (98%)
  between operations  0.64 us (1%)
    pallas_call x1, Pallas kernels, on_device(): pl.pallas_call(functools.partial(main_kernel, (ctx, chans, fast)), out_sh...  47.1 us
    pallas_call x1, Pallas kernels, on_device(): pl.pallas_call(final_kernel, out_shape=(like(1, tokens, width),) * 4 + (l...  1.23 us

profile of v5, /device:TPU:38, one launch (start us, length us, event | category | flops | bytes accessed | tf_op | source)
XLA Modules:
  0.0 49.0 jit_solution(2822699978179324760)
XLA Ops:
  0.6 47.1 %exchange.1 = (bf16[128,512]{1,0:T(8,128)(2,1)S(1)}, bf16[128,512]{1,0:T(8,128)(2,1)S(1)}, bf16[128,512]{1,0:T(8,128)(2,1)S(1)}, bf16[128,512]{1,0:T(8,128)(2,1)...) custom-call(bf16[128,512]{1,0:T(8,128)(2,1)} %filt_hbm.1, ...), custom_call_target="tpu_custom_call" | custom-call | tf_op jit(solution)/shard_map/exchange/pallas_call | solution.py:447
  47.8 1.2 %finish.1 = (bf16[1,128,512]{2,1,0:T(8,128)(2,1)}, bf16[1,128,512]{2,1,0:T(8,128)(2,1)}, bf16[1,128,512]{2,1,0:T(8,128)(2,1)}, bf16[1,128,512]{2,1,0:T(8,128)(2,1)}, bf16[128,512]{1,0:T(8,128)(2,1)}) custom-call(bf16[128,512]{1,0:T(8,128)(2,1)S(1)} %get-tuple-element.14.conv_ref, bf16[128,512]{1,0:T(8,128)(2,1)S(1)} %get-tuple-element.15.back_ref, ...), custom_call_target="tpu_custom_call" | custom-call | tf_op jit(solution)/shard_map/finish/pallas_call | solution.py:501

commit v6 on v5

--- a/solution.py
+++ b/solution.py
@@ -82,6 +82,7 @@
     head_send,
     head_recv,
     feat_next,
+    picks,
     heads_send,
     heads_recv,
     filt_send,
@@ -215,6 +216,13 @@
     by_channel = filt_ref[...].astype(F32).T.reshape(slow, fast, chans, tokens)
     filt_send[...] = by_channel.astype(BF16)
 
+    from_lane = lax.broadcasted_iota(jnp.int32, (tokens, width), 0)
+    to_chan = lax.broadcasted_iota(jnp.int32, (tokens, width), 1) % chans
+    for kind in range(2):
+        for position in range(2):
+            pick = from_lane == 2 * (to_chan + chans * kind) + position
+            picks[2 * kind + position] = jnp.where(pick, 1.0, 0.0).astype(BF16)
+
     pl.semaphore_wait(barrier, slow + fast + 1)
 
     rim_copy = remote(rim_send, rim_recv, 0, {"context": following})
@@ -228,33 +236,30 @@
 
     ring_scatter(filt_send, filt_mid, in_fast_ring, my_fast, fast, 1)
     rim_copy.wait()
-    head_copy.wait()
 
     keep = jnp.where(me == 0, 0.0, 1.0).astype(F32)
 
     def featured(rows_ref, which, start=8, count=None):
         if count is None:
             count = tokens
-            ext[8 : 8 + tokens] = rows_ref[...].astype(F32)
-            ext[6:8] = rim_recv[0, 2 * which : 2 * which + 2] * keep
+            ext[which, 8 : 8 + tokens] = rows_ref[...].astype(F32)
+            ext[which, 6:8] = rim_recv[0, 2 * which : 2 * which + 2] * keep
         total = None
         for lag in range(3):
             tap = taps[which, lag : lag + 1, :]
-            term = tap * ext[start - lag : start - lag + count]
+            term = tap * ext[which, start - lag : start - lag + count]
             total = term if total is None else total + term
         return total.astype(BF16)
 
     def featured_after(which):
-        ext[8 + tokens : 10 + tokens] = head_recv[0, 2 * which : 2 * which + 2]
+        ext[which, 8 + tokens : 10 + tokens] = head_recv[0, 2 * which : 2 * which + 2]
         return featured(None, which, 8 + tokens, 2).astype(F32)
 
     query_feat = featured(query_ref, 0)
     qf_out[...] = query_feat
     key_feat = featured(key_ref, 1)
-    feat_next[0:2] = featured_after(1)
     kf_out[...] = key_feat
     value_feat = featured(value_ref, 2)
-    feat_next[2:4] = featured_after(2)
     vf_out[...] = value_feat
     grad_out[...] = grad_ref[...]
     gated = (key_feat.astype(F32) * value_feat.astype(F32)).T.reshape(ctx, chans, tokens)
@@ -264,6 +269,9 @@
     scatter(pair_send, pair_recv, 2)
     wait_scatter(filt_mid, recv_sems, 1)
     ring_scatter(filt_mid, filt_recv, in_slow_ring, my_slow, slow, 7)
+    head_copy.wait()
+    feat_next[0:2] = featured_after(1)
+    feat_next[2:4] = featured_after(2)
 
     def spectra(wide_ref, rows, start, dest):
         for channel in range(chans):
@@ -357,14 +365,11 @@
 
     wait_scatter(heads_recv, recv_sems, 8)
     packed = heads_recv[...].reshape(ctx, tokens).astype(BF16)
-    from_lane = lax.broadcasted_iota(jnp.int32, (tokens, width), 0)
-    to_chan = lax.broadcasted_iota(jnp.int32, (tokens, width), 1) % chans
     holder = lax.broadcasted_iota(jnp.int32, (ctx, width), 0)
     is_mine = lax.broadcasted_iota(jnp.int32, (ctx, width), 1) // chans == holder
 
     def next_row(kind, position):
-        pick = from_lane == 2 * (to_chan + chans * kind) + position
-        spread = jnp.dot(packed, jnp.where(pick, 1.0, 0.0).astype(BF16), preferred_element_type=F32)
+        spread = jnp.dot(packed, picks[2 * kind + position], preferred_element_type=F32)
         return jnp.sum(jnp.where(is_mine, spread, 0.0), axis=0, keepdims=True)
 
     last_keep = jnp.where(me == ctx - 1, 0.0, 1.0).astype(F32)
@@ -462,12 +467,13 @@
         scratch_shapes=[
             *(buf(*x.shape, dtype=x.dtype) for x in operands[:-1]),
             buf(2 * ctx, tokens, dtype=F32),
-            buf(tokens + 16, width, dtype=F32),
+            buf(3, tokens + 16, width, dtype=F32),
             buf(1, 8, width, dtype=F32),
             buf(1, 8, width, dtype=F32),
             buf(1, 8, width, dtype=F32),
             buf(1, 8, width, dtype=F32),
             buf(8, width, dtype=F32),
+            buf(4, tokens, width),
             buf(ctx, 1, tokens, dtype=F32),
             buf(ctx, 1, tokens, dtype=F32),
             buf(slow, fast, chans, tokens),

time: 49.2 us -> 48.6 us (0.988)
  the two profiles are of different devices: /device:TPU:38 before, /device:TPU:112 now
where the time goes in v6:
time: 48.6 us; the launch traced here: 48.3 us
  Pallas kernels  47.7 us (98%)
  between operations  0.64 us (1%)
    pallas_call x1, Pallas kernels, on_device(): pl.pallas_call(functools.partial(main_kernel, (ctx, chans, fast)), out_sh...  46.5 us
    pallas_call x1, Pallas kernels, on_device(): pl.pallas_call(final_kernel, out_shape=(like(1, tokens, width),) * 4 + (l...  1.23 us

profile of v6, /device:TPU:112, one launch (start us, length us, event | category | flops | bytes accessed | tf_op | source)
XLA Modules:
  0.0 48.3 jit_solution(9239356171664264951)
XLA Ops:
  0.6 46.5 %exchange.1 = (bf16[128,512]{1,0:T(8,128)(2,1)S(1)}, bf16[128,512]{1,0:T(8,128)(2,1)S(1)}, bf16[128,512]{1,0:T(8,128)(2,1)S(1)}, bf16[128,512]{1,0:T(8,128)(2,1)...) custom-call(bf16[128,512]{1,0:T(8,128)(2,1)} %filt_hbm.1, ...), custom_call_target="tpu_custom_call" | custom-call | tf_op jit(solution)/shard_map/exchange/pallas_call | solution.py:452
  47.1 1.2 %finish.1 = (bf16[1,128,512]{2,1,0:T(8,128)(2,1)}, bf16[1,128,512]{2,1,0:T(8,128)(2,1)}, bf16[1,128,512]{2,1,0:T(8,128)(2,1)}, bf16[1,128,512]{2,1,0:T(8,128)(2,1)}, bf16[128,512]{1,0:T(8,128)(2,1)}) custom-call(bf16[128,512]{1,0:T(8,128)(2,1)S(1)} %get-tuple-element.14.conv_ref, bf16[128,512]{1,0:T(8,128)(2,1)S(1)} %get-tuple-element.15.back_ref, ...), custom_call_target="tpu_custom_call" | custom-call | tf_op jit(solution)/shard_map/finish/pallas_call | solution.py:507

commit v7 on v6

--- a/solution.py
+++ b/solution.py
@@ -171,14 +171,12 @@
 
     fast_places = [lax.rem(my_fast + offset, fast) for offset in far_offsets(fast)]
 
-    def scatter(src, dst, which, with_heads=False):
+    def scatter(src, dst, which):
         def send_row(row, count):
             base = row * fast
             for place in fast_places[:count]:
                 peer = base + place
                 remote(src.at[peer], dst.at[me], which, {"context": peer}).start()
-                if with_heads:
-                    remote(heads_send.at[peer], heads_recv.at[me], 8, {"context": peer}).start()
 
         @pl.loop(0, slow - 1)
         def _(step):
@@ -186,8 +184,6 @@
 
         send_row(my_slow, fast - 1)
         dst[me] = src[me]
-        if with_heads:
-            heads_recv[me] = heads_send[me]
 
     def ring_scatter(src, dst, place, mine, count, which):
         @pl.loop(0, count - 1)
@@ -348,7 +344,8 @@
     )
     heads_send[...] = pltpu.roll(sum(heads), ctx - 1, 0).reshape(ctx, 1, tokens)
     conv_send[...] = wide[...].reshape(ctx, 2 * chans, tokens).astype(BF16)
-    scatter(conv_send, conv_recv, 4, True)
+    scatter(conv_send, conv_recv, 4)
+    scatter(heads_send, heads_recv, 8)
     wait_scatter(lag_recv, recv_sems, 5)
     part_copy = remote(lag_recv, part_recv, 3, {"dp": partner})
     part_copy.start()

time: 48.6 us -> 50 us (1.029)
  Pallas kernels: 47.7 us -> 49.2 us
    pallas_call x1, Pallas kernels: 46.5 us -> 48 us  [on_device(): pl.pallas_call(functools.partial(main_kernel, (ctx, chans, fast)), out_sh...]
where the time goes in v7:
time: 50 us; the launch traced here: 49.9 us
  Pallas kernels  49.2 us (98%)
  between operations  0.64 us (1%)
    pallas_call x1, Pallas kernels, on_device(): pl.pallas_call(functools.partial(main_kernel, (ctx, chans, fast)), out_sh...  48 us
    pallas_call x1, Pallas kernels, on_device(): pl.pallas_call(final_kernel, out_shape=(like(1, tokens, width),) * 4 + (l...  1.23 us

profile of v7, /device:TPU:112, one launch (start us, length us, event | category | flops | bytes accessed | tf_op | source)
XLA Modules:
  0.0 49.9 jit_solution(12046895407295849110)
XLA Ops:
  0.6 48.0 %exchange.1 = (bf16[128,512]{1,0:T(8,128)(2,1)S(1)}, bf16[128,512]{1,0:T(8,128)(2,1)S(1)}, bf16[128,512]{1,0:T(8,128)(2,1)S(1)}, bf16[128,512]{1,0:T(8,128)(2,1)...) custom-call(bf16[128,512]{1,0:T(8,128)(2,1)} %filt_hbm.1, ...), custom_call_target="tpu_custom_call" | custom-call | tf_op jit(solution)/shard_map/exchange/pallas_call | solution.py:449
  48.6 1.2 %finish.1 = (bf16[1,128,512]{2,1,0:T(8,128)(2,1)}, bf16[1,128,512]{2,1,0:T(8,128)(2,1)}, bf16[1,128,512]{2,1,0:T(8,128)(2,1)}, bf16[1,128,512]{2,1,0:T(8,128)(2,1)}, bf16[128,512]{1,0:T(8,128)(2,1)}) custom-call(bf16[128,512]{1,0:T(8,128)(2,1)S(1)} %get-tuple-element.14.conv_ref, bf16[128,512]{1,0:T(8,128)(2,1)S(1)} %get-tuple-element.15.back_ref, ...), custom_call_target="tpu_custom_call" | custom-call | tf_op jit(solution)/shard_map/finish/pallas_call | solution.py:504
